TPU v7x, 512 devices: a whole 4x4x16 slice. The times are simulated.
512 devices in a mesh: row: 16 (over z_lo, x), col: 32 (over z_hi, y, core).
Axes of the slice: x: 4, y: 4, z: 16 (z_hi: 4, z_lo: 4; z = z_hi * 4 + z_lo), core: 2. Of those that a mesh axis runs over, the one named last changes fastest.
Arguments:
- features: bfloat16 [65536, 256], P(('row', 'col')), may hold values from -6 to 6
- adj_tiles: bfloat16 [16, 32, 96, 128, 128], P('row', 'col'), may hold values from -0.109375 to 0.109375
- tile_row: int32 [16, 32, 96], P('row', 'col'), may hold values from 0 to 31, as said below
- tile_col: int32 [16, 32, 96], P('row', 'col'), may hold values from 0 to 15
- tile_count: int32 [16, 32], P('row', 'col'), may hold values from 8 to 96, as said below
- w_self: bfloat16 [256, 256], replicated, may hold values from -0.375 to 0.375
- w_neigh: bfloat16 [256, 256], replicated, may hold values from -0.375 to 0.375
- bias_vec: float32 [256], replicated, may hold values from -3 to 3
- cotangent: bfloat16 [65536, 256], P(('row', 'col')), may hold values from -6 to 6
Outputs:
- layer_out: bfloat16 [65536, 256], P(('row', 'col'))
- grad_features: bfloat16 [65536, 256], P(('row', 'col'))
- grad_self: float32 [256, 256], replicated
- grad_neigh: float32 [256, 256], replicated
- grad_bias: float32 [256], replicated
Inputs may be any that keep to these rules, and one draw needn't show every extreme that they name: Within each block the 96 (tile_row, tile_col) pairs are distinct. `tile_count`: some block has all 96 slots occupied.
All inputs are finite; a program needn't handle non-finite values.
Results may differ from a plain program's by a relative error of at most 0.022.
Values may be sent and summed in bfloat16 or wider, within the bound.
A program may use at most 128 MiB of HBM per device.

v0:
```python
import jax
import jax.numpy as jnp
from jax import lax
from jax.sharding import PartitionSpec as P


def slot_products(tile_values, picked, forward):
    if forward:
        return jnp.einsum("tab,tbf->taf", tile_values, picked, preferred_element_type=jnp.float32)
    return jnp.einsum("tab,taf->tbf", tile_values, picked, preferred_element_type=jnp.float32)


def place_tiles(products, targets, occupied, segments):
    weighted = products * occupied[:, None, None]
    placed = (
        jnp.zeros((segments, products.shape[1], products.shape[2]), jnp.float32)
        .at[targets]
        .add(weighted)
    )
    return placed.reshape(segments * products.shape[1], products.shape[2])


def body(features, adj_tiles, tile_row, tile_col, tile_count, w_self, w_neigh, bias_vec, cotangent):
    tile_values = adj_tiles[0, 0]
    row_slots = tile_row[0, 0]
    col_slots = tile_col[0, 0]
    occupied = (jnp.arange(tile_values.shape[0]) < tile_count[0, 0]).astype(jnp.float32)
    order = tile_values.shape[1]
    own_nodes = features.shape[0]
    width_feat = features.shape[1]
    rows_count = lax.axis_size("row")
    cols_count = lax.axis_size("col")
    row_segments = own_nodes * cols_count // order
    col_segments = own_nodes * rows_count // order
    column_block = lax.all_gather(features, "row", axis=0, tiled=True)
    picked_cols = column_block.reshape(col_segments, order, width_feat)[col_slots]
    forward_terms = slot_products(tile_values, picked_cols, True)
    partial_rows = place_tiles(forward_terms, row_slots, occupied, row_segments)
    aggregate = lax.psum_scatter(
        partial_rows.astype(jnp.bfloat16), "col", scatter_dimension=0, tiled=True
    )
    preact = (
        jnp.dot(features, w_self, preferred_element_type=jnp.float32)
        + jnp.dot(aggregate, w_neigh, preferred_element_type=jnp.float32)
        + bias_vec
    )
    sigma = jax.nn.sigmoid(preact)
    layer_out = (preact * sigma).astype(jnp.bfloat16)
    grad_pre = cotangent.astype(jnp.float32) * sigma * (1.0 + preact * (1.0 - sigma))
    grad_pre_b = grad_pre.astype(jnp.bfloat16)
    neigh_grad = jnp.dot(grad_pre_b, w_neigh.T, preferred_element_type=jnp.float32).astype(
        jnp.bfloat16
    )
    row_block = lax.all_gather(neigh_grad, "col", axis=0, tiled=True)
    picked_rows = row_block.reshape(row_segments, order, width_feat)[row_slots]
    backward_terms = slot_products(tile_values, picked_rows, False)
    partial_cols = place_tiles(backward_terms, col_slots, occupied, col_segments)
    back_share = lax.psum_scatter(
        partial_cols.astype(jnp.bfloat16), "row", scatter_dimension=0, tiled=True
    ).astype(jnp.float32)
    grad_features = (
        jnp.dot(grad_pre_b, w_self.T, preferred_element_type=jnp.float32) + back_share
    ).astype(jnp.bfloat16)
    contract = (((0,), (0,)), ((), ()))
    self_term = lax.dot_general(features, grad_pre_b, contract, preferred_element_type=jnp.float32)
    neigh_term = lax.dot_general(
        aggregate, grad_pre_b, contract, preferred_element_type=jnp.float32
    )
    bias_term = jnp.sum(grad_pre, axis=0)
    grad_self, grad_neigh, grad_bias = lax.psum((self_term, neigh_term, bias_term), ("row", "col"))
    factor = 1.0 / jnp.sqrt(jnp.float32(own_nodes * rows_count * cols_count))
    return (layer_out, grad_features, grad_self * factor, grad_neigh * factor, grad_bias * factor)


def solution(mesh):
    placed = (
        P(("row", "col"), None),
        P("row", "col", None, None, None),
        P("row", "col", None),
        P("row", "col", None),
        P("row", "col"),
        P(),
        P(),
        P(),
        P(("row", "col"), None),
    )
    return jax.shard_map(
        body,
        mesh=mesh,
        in_specs=placed,
        out_specs=(P(("row", "col"), None), P(("row", "col"), None), P(), P(), P()),
        check_vma=False,
    )
```

profile of v0, /device:TPU:1, one launch (start us, length us, event | category | flops | bytes accessed | tf_op | source)
XLA Modules:
  0.0 909.8 jit_solution(13270558118492989166)
XLA Ops:
  7.2 0.0 copy-start
  7.2 0.0 all-gather.3.cloned.1.call-start
  7.2 0.7 all-gather.3.cloned.1.call-update
  7.9 0.0 reduce-scatter.3.cloned.1.call-start
  8.8 0.7 fusion.5
  9.5 0.7 fusion.4
  10.1 81.6 %all-gather.3.cloned.1.call-done = bf16[2048,256]{1,0:T(8,128)(2,1)} async-done(((bf16[128,256]{1,0:T(8,128)(2,1)}), bf16[2048,256]{1,0:T(8,128)(2,1)}) %all-gather.3.cloned.1.call-update) | async-done | bytes 1048592 | tf_op jit(solution)/shard_map/all_gather | solution.py:35
  91.7 7.2 gather_fusion
  98.9 0.0 copy-done
  98.9 9.8 %multiply_bitcast_fusion.1 = f32[96,128,256]{1,2,0:T(8,128)} fusion(f32[96]{0:T(128)S(1)} %compare_convert_fusion, bf16[96,128,256]{2,1,0:T(8,128)(2,1)} %gather_fusion, bf16[1,1,96,128,128]{4,3,2,1,0:T(8,128)(2,1)S(1)} %copy-done), kind=kOutput, calls=%fused_computation.5 | convolution fusion | flops 808452096 | bytes 22020480 | tf_op jit(solution)/shard_map/tab,tbf->taf/dot_general | solution.py:9
  108.8 12.6 %copy.20 = f32[96,128,256]{2,1,0:T(8,128)} copy(f32[96,128,256]{1,2,0:T(8,128)} %multiply_bitcast_fusion.1) | data formatting | bytes 25165824 | tf_op jit(solution)/shard_map/mul | solution.py:14
  121.3 2.4 broadcast_in_dim.4
  123.8 28.4 %scatter_fusion = f32[32,128,256]{2,1,0:T(8,128)} fusion(f32[32,128,256]{2,1,0:T(8,128)} %broadcast_in_dim.4, s32[96]{0:T(128)S(1)} %fusion.4, f32[96,128,256]{2,1,0:T(8,128)} %copy.20), kind=kCustom, calls=%fused_computation.2 | custom fusion | flops 3145728 | bytes 37749120 | tf_op jit(solution)/shard_map/scatter-add | solution.py:18
  152.1 0.0 copy-start.1
  152.1 0.0 copy-start.2
  152.1 0.0 copy-start.3
  152.1 0.0 copy-start.4
  152.2 3.9 convert_element_type.38
  156.0 0.0 reduce-scatter.3.cloned.1.call-update
  156.0 0.0 all-gather.5.cloned.1.call-start
  156.1 0.0 copy-done.1
  156.1 0.0 copy-done.2
  156.1 0.8 fusion.7
  156.9 128.6 %reduce-scatter.3.cloned.1.call-done = bf16[128,256]{1,0:T(8,128)(2,1)} async-done(((bf16[4096,256]{1,0:T(8,128)(2,1)}), bf16[128,256]{1,0:T(8,128)(2,1)}) %reduce-scatter.3.cloned.1.call-update) | async-done | bytes 65552 | tf_op jit(solution)/shard_map/reduce_scatter | solution.py:39
  285.5 0.0 copy-done.3
  285.5 0.0 copy-done.4
  285.5 1.9 fusion.6
  287.3 1.7 convolution_convert_fusion
  289.1 0.0 all-gather.5.cloned.1.call-update
  289.1 0.0 all-reduce.3.cloned.1.call-start
  289.2 0.9 convolution_bitcast_fusion
  290.1 1.8 fusion.8
  291.9 0.0 all-reduce.3.cloned.1.call-update
  291.9 0.2 reduce-scatter.5.cloned.1.call-start
  292.1 71.1 %all-gather.5.cloned.1.call-done = bf16[4096,256]{1,0:T(8,128)(2,1)} async-done(((bf16[128,256]{1,0:T(8,128)(2,1)}), bf16[4096,256]{1,0:T(8,128)(2,1)}) %all-gather.5.cloned.1.call-update) | async-done | bytes 2097168 | tf_op jit(solution)/shard_map/all_gather | solution.py:54
  363.2 7.6 gather_fusion.1
  370.8 9.8 %multiply_bitcast_fusion = f32[96,128,256]{1,2,0:T(8,128)} fusion(f32[96]{0:T(128)S(1)} %compare_convert_fusion, bf16[96,128,256]{2,1,0:T(8,128)(2,1)} %gather_fusion.1, bf16[1,1,96,128,128]{4,3,2,1,0:T(8,128)(2,1)S(1)} %copy-done), kind=kOutput, calls=%fused_computation.4 | convolution fusion | flops 808452096 | bytes 22020480 | tf_op jit(solution)/shard_map/tab,taf->tbf/dot_general | solution.py:10
  380.6 12.6 %copy.22 = f32[96,128,256]{2,1,0:T(8,128)} copy(f32[96,128,256]{1,2,0:T(8,128)} %multiply_bitcast_fusion) | data formatting | bytes 25165824 | tf_op jit(solution)/shard_map/mul | solution.py:14
  393.2 1.5 broadcast_in_dim.5
  394.7 28.2 %scatter_fusion.1 = f32[16,128,256]{2,1,0:T(8,128)} fusion(f32[16,128,256]{2,1,0:T(8,128)} %broadcast_in_dim.5, s32[96]{0:T(128)S(1)} %fusion.5, f32[96,128,256]{2,1,0:T(8,128)} %copy.22), kind=kCustom, calls=%fused_computation.3 | custom fusion | flops 3145728 | bytes 37749120 | tf_op jit(solution)/shard_map/scatter-add | solution.py:18
  423.0 2.7 convert_element_type.44
  425.7 0.0 reduce-scatter.5.cloned.1.call-update
  425.7 102.6 %psum.23 = f32[256]{0:T(256)S(1)} all-reduce(f32[256]{0:T(256)S(1)} %get-tuple-element.17), channel_id=1, replica_groups=mesh['row'=16,'col'=32] {'row','col'}, use_global_device_ids=true, to_apply=%region_7.0 | all-reduce | flops 256 | bytes 2048 | tf_op jit(solution)/shard_map/psum | solution.py:70
  528.3 0.6 broadcast_multiply_fusion.2
  528.9 293.2 %all-reduce.3.cloned.1.call-done = (f32[256,256]{0,1:T(8,128)}, f32[256,256]{0,1:T(8,128)}) async-done(((f32[256,256]{0,1:T(8,128)}, f32[256,256]{0,1:T(8,128)}), (f32[256,256]{0,1:T(8,128)}, f32[256,256]{0,1:T(8,128)})) %all-reduce.3.cloned.1.call-update) | async-done | bytes 524304 | tf_op jit(solution)/shard_map/psum | solution.py:70
  822.1 1.8 broadcast_multiply_fusion
  823.9 1.8 copy.24
  825.7 0.8 copy.25
  826.5 75.0 %reduce-scatter.5.cloned.1.call-done = bf16[128,256]{1,0:T(8,128)(2,1)} async-done(((bf16[2048,256]{1,0:T(8,128)(2,1)}), bf16[128,256]{1,0:T(8,128)(2,1)}) %reduce-scatter.5.cloned.1.call-update) | async-done | bytes 65552 | tf_op jit(solution)/shard_map/reduce_scatter | solution.py:58
  901.5 1.7 fusion.3
  (3 shorter events, 0.0 us)
Async XLA Ops:
  7.2 91.8 %copy-start = (bf16[1,1,96,128,128]{4,3,2,1,0:T(8,128)(2,1)S(1)}, bf16[1,1,96,128,128]{4,3,2,1,0:T(8,128)(2,1)}, u32[]{:S(2)}) copy-start(bf16[1,1,96,128,128]{4,3,2,1,0:T(8,128)(2,1)} %param.10) | copy-start | bytes 9437188
  7.2 84.5 %all-gather.3.cloned.1.call-start = ((), (), s32[]{:S(2)}) async-start(), calls=%async_computation.2 | async-start | bytes 1114112 | tf_op jit(solution)/shard_map/all_gather | solution.py:35
  7.9 277.6 %reduce-scatter.3.cloned.1.call-start = ((), (), s32[]{:S(2)}) async-start(), calls=%async_computation.3 | async-start | bytes 2162688 | tf_op jit(solution)/shard_map/reduce_scatter | solution.py:39
  152.1 3.9 copy-start.1
  152.1 4.0 copy-start.2
  152.1 133.3 %copy-start.3 = (bf16[128,256]{1,0:T(8,128)(2,1)S(1)}, bf16[128,256]{1,0:T(8,128)(2,1)}, u32[]{:S(2)}) copy-start(bf16[128,256]{1,0:T(8,128)(2,1)} %param.17) | copy-start | bytes 196612
  152.1 133.3 %copy-start.4 = (f32[256]{0:T(256)S(1)}, f32[256]{0:T(256)}, u32[]{:S(2)}) copy-start(f32[256]{0:T(256)} %param.16) | copy-start | bytes 3076
  156.0 207.2 %all-gather.5.cloned.1.call-start = ((), (), s32[]{:S(2)}) async-start(), calls=%async_computation.4 | async-start | bytes 2162688 | tf_op jit(solution)/shard_map/all_gather | solution.py:54
  289.1 533.0 %all-reduce.3.cloned.1.call-start = ((), (), s32[]{:S(2)}) async-start(), calls=%async_computation.6 | async-start | bytes 1048576 | tf_op jit(solution)/shard_map/psum | solution.py:70
  291.9 609.7 %reduce-scatter.5.cloned.1.call-start = ((), (), s32[]{:S(2)}) async-start(), calls=%async_computation.5 | async-start | bytes 1114112 | tf_op jit(solution)/shard_map/reduce_scatter | solution.py:58
Sparse Core Ops, SparseCore 0:
  10.1 81.5 all-gather.2
  156.2 129.2 reduce-scatter.2
  289.2 73.9 all-gather.4
  369.1 452.9 all-reduce.2
  825.0 76.4 reduce-scatter.4
where the time goes:
time: 921 us; the launch traced here: 910 us
  waiting for transfers between devices  650 us (71%)
  blocking collectives  103 us (11%)
  other arithmetic  66.8 us (7%)
  local copies, waits for them, and re-layouts  46.5 us (5%)
  matrix products  28.5 us (3%)
  between operations  14.6 us (2%)
    psum x1, waiting for transfers between devices, body(): lax.psum((self_term, neigh_term, bias_term), ('row', 'col'))  293 us
    reduce_scatter x1, waiting for transfers between devices, body(): lax.psum_scatter(partial_rows.astype(jnp.bfloat16), 'col', scatter_dimens...  129 us
    psum x1, blocking collectives, body(): lax.psum((self_term, neigh_term, bias_term), ('row', 'col'))  103 us
    all_gather x1, waiting for transfers between devices, body(): column_block = lax.all_gather(features, 'row', axis=0, tiled=True)  81.6 us
    reduce_scatter x1, waiting for transfers between devices, body(): lax.psum_scatter(partial_cols.astype(jnp.bfloat16), 'row', scatter_dimens...  75 us
    all_gather x1, waiting for transfers between devices, body(): row_block = lax.all_gather(neigh_grad, 'col', axis=0, tiled=True)  71.1 us
    scatter-add x2, other arithmetic, place_tiles(): placed = jnp.zeros((segments, products.shape[1], products.shape[2]), jnp....  56.6 us
    mul x2, local copies, waits for them, and re-layouts, place_tiles(): weighted = products * occupied[:, None, None]  25.2 us
  transfers between devices with their start and end apart: 5, of which 5 were waited for; matrix products, arithmetic and copies ran while one was open for 8% of the time, Pallas kernels for 0%

commit v1 on v0

v1 whole, which is shorter than its diff:
```python
import jax
import jax.numpy as jnp
from jax import lax
from jax.experimental import pallas as pl
from jax.experimental.pallas import tpu as pltpu
from jax.sharding import PartitionSpec as P

MESH = pl.DeviceIdType.MESH
BF = jnp.bfloat16
F32 = jnp.float32
SLOTS = 96
ZERO = SLOTS
TN = (((0,), (0,)), ((), ()))
NT = (((1,), (1,)), ((), ()))
Z_FAR = (2, 1, 3, 0)
Z_NEAR = (0, 1, 3, 2)
RING = (1, 3, 2)


def mod4(v):
    return lax.rem(v, 4)


def dot(a, b):
    return jnp.dot(a, b, preferred_element_type=F32)


def kernel(
    inv, feat, tiles, w_self, w_neigh, bias, cot,
    out, gfeat, gself, gneigh, gbias,
    A, T, X, PA, CR, Y, YR, ZS, ZR, G, ACC, BP, XR, XS, LR,
    W, M, MC, M1, MX, M2, MY, M3, ML, M4, MH, R,
    tsem, s1z, r1z, s1x, r1x, s3c, r3c, s3y, r3y, s3z, r3z,
    s5z, r5z, s5y, r5y, s5c, r5c, s6x, r6x, s6l, r6l, sw, rw,
):
    i = lax.axis_index("row")
    j = lax.axis_index("col")
    zl, x = lax.div(i, 4), lax.rem(i, 4)
    zh, yc = lax.div(j, 8), lax.rem(j, 8)
    y, c = lax.div(yc, 2), lax.rem(yc, 2)
    oc = 1 - c

    def partner(d):
        if d == 0:
            return zl
        if d == 1:
            return zl + 1 - 2 * lax.rem(zl, 2)
        if d == 2:
            return mod4(zl + 2)
        return 3 - zl

    def dev(zl_=zl, x_=x, zh_=zh, y_=y, c_=c):
        return (zl_ * 4 + x_, zh_ * 8 + y_ * 2 + c_)

    sent = []

    def send(src, dst, ssem, rsem, device):
        copy = pltpu.make_async_remote_copy(
            src_ref=src, dst_ref=dst, send_sem=ssem, recv_sem=rsem, device_id=device, device_id_type=MESH
        )
        copy.start()
        sent.append(copy)
        return copy

    load = pltpu.make_async_copy(tiles.at[0, 0], T.at[pl.ds(0, SLOTS)], tsem)
    load.start()

    barrier = pltpu.get_barrier_semaphore()
    peers = [dev(c_=oc)]
    for d in (1, 2, 3):
        peers += [dev(zl_=partner(d)), dev(x_=mod4(x + d)), dev(y_=mod4(y + d)), dev(zh_=mod4(zh + d))]
    for peer in peers:
        pl.semaphore_signal(barrier, inc=1, device_id=peer, device_id_type=MESH)
    pl.semaphore_wait(barrier, len(peers))

    z_in = {d: send(feat, X.at[i], s1z.at[d - 1], r1z.at[d - 1], dev(zl_=partner(d))) for d in (1, 2, 3)}
    x_in = []
    for d in RING:
        x_in.append(send(feat, X.at[i], s1x.at[0, d - 1], r1x.at[0, d - 1], dev(x_=mod4(x + d))))
    X[i] = feat[...]
    T[ZERO] = jnp.zeros((128, 128), BF)
    load.wait()

    def densify(first, count):
        @pl.loop(first, first + count)
        def _(p):
            rows = pl.ds(pl.multiple_of(p * 128, 128), 128)
            for q in range(16):
                A[rows, q * 128 : (q + 1) * 128] = T[inv[p * 16 + q]]

    densify(0, 11)
    for d in (1, 2, 3):
        z_in[d].wait_recv()
        block = X.at[partner(d) * 4 + x]
        for e in RING:
            x_in.append(send(block, block, s1x.at[d, e - 1], r1x.at[d, e - 1], dev(x_=mod4(x + e))))
        densify(4 + 7 * d, 7)
    own_term = dot(feat[...], w_self[...]) + bias[...]
    for copy in x_in:
        copy.wait_recv()

    core_in, y_in, zr_in = {}, {}, {}

    def after_core(n):
        zq = mod4(zh + Z_FAR[n])
        core_in[n].wait_recv()
        Y[zq] = (PA[zq, c].astype(F32) + CR[n].astype(F32)).astype(BF)
        y_in[n] = [
            send(Y.at[zq, mod4(y + d)], YR.at[n, d - 1], s3y.at[n, d - 1], r3y.at[n, d - 1], dev(y_=mod4(y + d)))
            for d in RING
        ]

    for n in range(4):
        zq = mod4(zh + Z_FAR[n])
        rows = pl.ds(pl.multiple_of(zq * 1024, 1024), 1024)
        PA[zq] = dot(A[rows, :], X[...].reshape(2048, 256)).astype(BF).reshape(2, 4, 128, 256)
        core_in[n] = send(PA.at[zq, oc], CR.at[n], s3c.at[n], r3c.at[n], dev(c_=oc))
        if n:
            after_core(n - 1)
    after_core(3)
    for n in range(4):
        zq = mod4(zh + Z_FAR[n])
        for copy in y_in[n]:
            copy.wait_recv()
        total = Y[zq, y].astype(F32)
        for d in range(3):
            total = total + YR[n, d].astype(F32)
        if n < 3:
            ZS[n] = total.astype(BF)
            dz = Z_FAR[n]
            zr_in[dz] = send(ZS.at[n], ZR.at[dz - 1], s3z.at[dz - 1], r3z.at[dz - 1], dev(zh_=mod4(zh + dz)))
    for dz in RING:
        zr_in[dz].wait_recv()
        total = total + ZR[dz - 1].astype(F32)
    aggregate = total.astype(BF)

    preact = own_term + dot(aggregate, w_neigh[...])
    sigma = jax.nn.sigmoid(preact)
    out[...] = (preact * sigma).astype(BF)
    grad_pre = cot[...].astype(F32) * sigma * (1.0 + preact * (1.0 - sigma))
    grad_pre_b = grad_pre.astype(BF)
    G[zh, c, y] = lax.dot_general(grad_pre_b, w_neigh[...], NT, preferred_element_type=F32).astype(BF)

    own = G.at[zh, c, y]
    gz_in = {dz: send(own, own, s5z.at[dz - 1], r5z.at[dz - 1], dev(zh_=mod4(zh + dz))) for dz in (2, 1, 3)}
    gy_in, gc_in = {}, {}

    def send_y(dz):
        block = G.at[mod4(zh + 4 - dz), c, y]
        gy_in[dz] = [
            send(block, block, s5y.at[dz, d - 1], r5y.at[dz, d - 1], dev(y_=mod4(y + d))) for d in RING
        ]

    def send_core(dz):
        for copy in gy_in[dz]:
            copy.wait_recv()
        slab = G.at[mod4(zh + 4 - dz), c]
        gc_in[dz] = send(slab, slab, s5c.at[dz], r5c.at[dz], dev(c_=oc))

    def back(dz, part):
        zq = mod4(zh + 4 - dz)
        rows = pl.ds(pl.multiple_of(zq * 1024, 1024), 1024)
        columns = pl.ds(pl.multiple_of(part * 512, 512), 512)
        return lax.dot_general(A[rows, columns], G[zq].reshape(1024, 256), TN, preferred_element_type=F32)

    def back_all(dz, first):
        gc_in[dz].wait_recv()

        @pl.loop(0, 4)
        def _(part):
            if first:
                ACC[part] = back(dz, part)
            else:
                ACC[part] += back(dz, part)

    send_y(0)

    W[0:256] = lax.dot_general(feat[...], grad_pre_b, TN, preferred_element_type=F32)
    W[256:512] = lax.dot_general(aggregate, grad_pre_b, TN, preferred_element_type=F32)
    ones = jnp.sum(grad_pre, axis=0, keepdims=True)
    row_id = lax.broadcasted_iota(jnp.int32, (8, 128), 0)
    bias_tile = jnp.where(row_id == 0, ones[:, :128], jnp.where(row_id == 1, ones[:, 128:], 0.0))
    gpw = lax.dot_general(grad_pre_b, w_self[...], NT, preferred_element_type=F32)

    @pl.loop(0, 32)
    def _(q):
        rows = W[pl.ds(pl.multiple_of(q * 16, 16), 16), :]
        a, b = lax.div(q, 16), lax.rem(q, 16)
        u, v = lax.div(b, 4), lax.rem(b, 4)
        M[a, u, v, 0] = rows[0:8, 0:128]
        M[a, u, v, 1] = rows[0:8, 128:256]
        M[a, u, v, 2] = rows[8:16, 0:128]
        M[a, u, v, 3] = rows[8:16, 128:256]
        M[a, u, v, 4] = bias_tile

    wc = send(M.at[oc], MC, sw.at[0], rw.at[0], dev(c_=oc))
    wc.wait_recv()
    M1[...] = M[c] + MC[...]
    wx = [send(M1.at[mod4(x + d)], MX.at[d - 1], sw.at[d], rw.at[d], dev(x_=mod4(x + d))) for d in RING]

    gz_in[1].wait_recv()
    send_y(1)
    gz_in[3].wait_recv()
    send_y(3)
    send_core(0)
    for copy in wx:
        copy.wait_recv()
    M2[...] = M1[x] + MX[0] + MX[1] + MX[2]
    wy = [send(M2.at[mod4(y + d)], MY.at[d - 1], sw.at[3 + d], rw.at[3 + d], dev(y_=mod4(y + d))) for d in RING]
    gz_in[2].wait_recv()
    send_y(2)
    back_all(0, True)
    send_core(1)
    for copy in wy:
        copy.wait_recv()
    M3[...] = M2[y] + MY[0] + MY[1] + MY[2]
    wl = [send(M3, ML.at[d - 1], sw.at[6 + d], rw.at[6 + d], dev(zl_=partner(d))) for d in (1, 2, 3)]
    send_core(3)
    back_all(1, False)
    for copy in wl:
        copy.wait_recv()
    M4[...] = M3[...] + ML[0] + ML[1] + ML[2]
    wh = [send(M4, MH.at[d - 1], sw.at[9 + d], rw.at[9 + d], dev(zh_=mod4(zh + d))) for d in (2, 1, 3)]
    back_all(3, False)
    send_core(2)
    gc_in[2].wait_recv()

    x6, l6 = [], {}
    for n in range(4):
        part = partner(3 - n)
        BP[part] = (ACC[part] + back(2, part)).astype(BF).reshape(4, 128, 256)
        x6.append([
            send(BP.at[part, mod4(x + d)], XR.at[n, d - 1], s6x.at[n, d - 1], r6x.at[n, d - 1], dev(x_=mod4(x + d)))
            for d in RING
        ])

    def after_x(n):
        d = 3 - n
        part = partner(d)
        for copy in x6[n]:
            copy.wait_recv()
        total = BP[part, x].astype(F32)
        for e in range(3):
            total = total + XR[n, e].astype(F32)
        if d:
            XS[n] = total.astype(BF)
            l6[d] = send(XS.at[n], LR.at[d - 1], s6l.at[d - 1], r6l.at[d - 1], dev(zl_=partner(d)))
        return total

    for copy in wh:
        copy.wait_recv()
    sums = M4[...] + (MH[0] + MH[1] + MH[2])
    R[c, x, y] = sums[0:4]
    block = R.at[c, x, y]
    vy = [send(block, block, sw.at[12 + d], rw.at[12 + d], dev(y_=mod4(y + d))) for d in RING]
    after_x(0)
    after_x(1)
    for copy in vy:
        copy.wait_recv()
    slab = R.at[c, x]
    vx = [send(slab, slab, sw.at[15 + d], rw.at[15 + d], dev(x_=mod4(x + d))) for d in RING]
    after_x(2)
    total = after_x(3)
    for copy in vx:
        copy.wait_recv()
    half = R.at[c]
    vc = send(half, half, sw.at[19], rw.at[19], dev(c_=oc))
    for d in (1, 2, 3):
        l6[d].wait_recv()
        total = total + LR[d - 1].astype(F32)
    gfeat[...] = (total + gpw).astype(BF)
    factor = 1.0 / 256.0
    gbias[...] = sums[4] * factor
    vc.wait_recv()

    @pl.loop(0, 16)
    def _(q):
        rows = pl.ds(pl.multiple_of(q * 16, 16), 16)
        u, v = lax.div(q, 4), lax.rem(q, 4)
        for a, ref in ((0, gself), (1, gneigh)):
            upper = jnp.concatenate([R[a, u, v, 0], R[a, u, v, 1]], axis=1)
            lower = jnp.concatenate([R[a, u, v, 2], R[a, u, v, 3]], axis=1)
            ref[rows, :] = jnp.concatenate([upper, lower], axis=0) * factor

    for copy in sent:
        copy.wait_send()


def body(features, adj_tiles, tile_row, tile_col, tile_count, w_self, w_neigh, bias_vec, cotangent):
    rows, cols = tile_row[0, 0], tile_col[0, 0]
    placed = (rows // 8) * 8 + (rows % 2) * 4 + (rows % 8) // 2
    where = placed * 16 + cols
    slot = jnp.arange(SLOTS, dtype=jnp.int32)
    hit = (where[:, None] == jnp.arange(512, dtype=jnp.int32)[None, :]) & (slot < tile_count[0, 0])[:, None]
    inv = jnp.min(jnp.where(hit, slot[:, None], ZERO), axis=0)
    vmem = pl.BlockSpec(memory_space=pltpu.VMEM)
    dma = pltpu.SemaphoreType.DMA
    sds = jax.ShapeDtypeStruct
    out, gfeat, gself, gneigh, gbias = pl.pallas_call(
        kernel,
        out_shape=(
            sds((128, 256), BF), sds((128, 256), BF), sds((256, 256), F32), sds((256, 256), F32), sds((8, 128), F32),
        ),
        in_specs=[
            pl.BlockSpec(memory_space=pltpu.SMEM), vmem, pl.BlockSpec(memory_space=pl.ANY), vmem, vmem, vmem, vmem,
        ],
        out_specs=(vmem,) * 5,
        scratch_shapes=[
            pltpu.VMEM((4096, 2048), BF),
            pltpu.VMEM((SLOTS + 1, 128, 128), BF),
            pltpu.VMEM((16, 128, 256), BF),
            pltpu.VMEM((4, 2, 4, 128, 256), BF),
            pltpu.VMEM((4, 4, 128, 256), BF),
            pltpu.VMEM((4, 4, 128, 256), BF),
            pltpu.VMEM((4, 3, 128, 256), BF),
            pltpu.VMEM((3, 128, 256), BF),
            pltpu.VMEM((3, 128, 256), BF),
            pltpu.VMEM((4, 2, 4, 128, 256), BF),
            pltpu.VMEM((4, 512, 256), F32),
            pltpu.VMEM((4, 4, 128, 256), BF),
            pltpu.VMEM((4, 3, 128, 256), BF),
            pltpu.VMEM((3, 128, 256), BF),
            pltpu.VMEM((3, 128, 256), BF),
            pltpu.VMEM((512, 256), F32),
            pltpu.VMEM((2, 4, 4, 5, 8, 128), F32),
            pltpu.VMEM((4, 4, 5, 8, 128), F32),
            pltpu.VMEM((4, 4, 5, 8, 128), F32),
            pltpu.VMEM((3, 4, 5, 8, 128), F32),
            pltpu.VMEM((4, 5, 8, 128), F32),
            pltpu.VMEM((3, 5, 8, 128), F32),
            pltpu.VMEM((5, 8, 128), F32),
            pltpu.VMEM((3, 5, 8, 128), F32),
            pltpu.VMEM((5, 8, 128), F32),
            pltpu.VMEM((3, 5, 8, 128), F32),
            pltpu.VMEM((2, 4, 4, 4, 8, 128), F32),
            dma,
            dma((3,)), dma((3,)), dma((4, 3)), dma((4, 3)),
            dma((4,)), dma((4,)), dma((4, 3)), dma((4, 3)), dma((3,)), dma((3,)),
            dma((3,)), dma((3,)), dma((4, 3)), dma((4, 3)), dma((4,)), dma((4,)),
            dma((4, 3)), dma((4, 3)), dma((3,)), dma((3,)),
            dma((20,)), dma((20,)),
        ],
        compiler_params=pltpu.CompilerParams(
            collective_id=0, has_side_effects=True, vmem_limit_bytes=56 * 2**20
        ),
    )(inv, features, adj_tiles, w_self, w_neigh, bias_vec.reshape(1, 256), cotangent)
    return out, gfeat, gself, gneigh, gbias[0:2].reshape(256)


def solution(mesh):
    placed = (
        P(("row", "col"), None),
        P("row", "col", None, None, None),
        P("row", "col", None),
        P("row", "col", None),
        P("row", "col"),
        P(),
        P(),
        P(),
        P(("row", "col"), None),
    )
    return jax.shard_map(
        body,
        mesh=mesh,
        in_specs=placed,
        out_specs=(P(("row", "col"), None), P(("row", "col"), None), P(), P(), P()),
        check_vma=False,
    )
```

time: 921 us -> 120 us (0.13); the launches traced: 910 us -> 119 us
  waiting for transfers between devices: 650 us -> 0 us
  Pallas kernels: 0 us -> 109 us
  blocking collectives: 103 us -> 0 us
  other arithmetic: 66.8 us -> 1.4 us
  local copies, waits for them, and re-layouts: 46.5 us -> 7.51 us
  matrix products: 28.5 us -> 0 us
  between operations: 14.6 us -> 1.3 us
    psum x1 -> x0, waiting for transfers between devices: 293 us -> none  [body(): lax.psum((self_term, neigh_term, bias_term), ('row', 'col'))]
    reduce_scatter x2 -> x0, waiting for transfers between devices: 204 us -> none  [the longest x1 129 us: body(): lax.psum_scatter(partial_rows.astype(jnp.bfloat16), 'col', scatter_dimens...]
    all_gather x2 -> x0, waiting for transfers between devices: 153 us -> none  [the longest x1 81.6 us: body(): column_block = lax.all_gather(features, 'row', axis=0, tiled=True)]
    pallas_call x0 -> x1, Pallas kernels: none -> 109 us  [body(): pl.pallas_call(kernel, out_shape=(sds((128, 256), BF), sds((128, 256), BF...]
    psum x1 -> x0, blocking collectives: 103 us -> none  [body(): lax.psum((self_term, neigh_term, bias_term), ('row', 'col'))]
    scatter-add x2 -> x0, other arithmetic: 56.6 us -> none  [place_tiles(): placed = jnp.zeros((segments, products.shape[1], products.shape[2]), jnp....]
    dot_general x8 -> x0, matrix products: 28.5 us -> none  [the longest x1 9.85 us: slot_products(): jnp.einsum('tab,tbf->taf', tile_values, picked, preferred_element_type=jn...]
    mul x2 -> x0, local copies, waits for them, and re-layouts: 25.2 us -> none  [place_tiles(): weighted = products * occupied[:, None, None]]
  transfers between devices with their start and end apart: 5 -> 0, of which waited for: 5 -> 0; matrix products, arithmetic and copies ran while one was open for 8% -> 0% of each run, Pallas kernels for 0% -> 0%
where the time goes in v1:
time: 120 us; the launch traced here: 119 us
  Pallas kernels  109 us (91%)
  local copies, waits for them, and re-layouts  7.51 us (6%)
  other arithmetic  1.4 us (1%)
  between operations  1.3 us (1%)
    pallas_call x1, Pallas kernels, body(): pl.pallas_call(kernel, out_shape=(sds((128, 256), BF), sds((128, 256), BF...  109 us
    unnamed x4, local copies, waits for them, and re-layouts  6.28 us

profile of v1, /device:TPU:1, one launch (start us, length us, event | category | flops | bytes accessed | tf_op | source)
XLA Modules:
  0.0 119.4 jit_solution(3637276765968076404)
XLA Ops:
  1.3 0.7 bitcast_add_fusion
  2.0 0.7 select_reduce_fusion.inv
  2.7 109.2 %shard_map.128 = (bf16[128,256]{1,0:T(8,128)(2,1)}, bf16[128,256]{1,0:T(8,128)(2,1)}, f32[256,256]{1,0:T(8,128)}, f32[256,256]{1,0:T(8,128)}, f32[8,128]{1,0:T(8,128)}) custom-call(s32[512]{0:T(512)} %select_reduce_fusion.inv, bf16[128,256]{1,0:T(8,128)(2,1)} %feat.1, bf16[1,1,96,128,128]{4,3,2,1,0:T(8,128)(2,1)} %tiles.1, bf16[256,256]{1,0:T(8,128)(2,1)} %w_self.1, ...), custom_call_target="tpu_custom_call" | custom-call | tf_op jit(solution)/shard_map/pallas_call | solution.py:299
  111.9 1.2 %slice_bitcast_fusion = f32[256]{0:T(256)} fusion(f32[8,128]{1,0:T(8,128)} %get-tuple-element.14), kind=kLoop, calls=%fused_computation.10 | loop fusion | bytes 2048 | tf_op jit(solution)/shard_map/reshape | solution.py:347
  113.1 1.5 %copy.19 = bf16[128,256]{1,0:T(8,128)(2,1)} copy(bf16[128,256]{1,0:T(8,128)(2,1)} %get-tuple-element.20) | data formatting | bytes 131072
  114.6 1.5 %copy.20 = bf16[128,256]{1,0:T(8,128)(2,1)} copy(bf16[128,256]{1,0:T(8,128)(2,1)} %get-tuple-element.21) | data formatting | bytes 131072
  116.1 1.7 %copy.21 = f32[256,256]{1,0:T(8,128)} copy(f32[256,256]{1,0:T(8,128)} %get-tuple-element.22) | data formatting | bytes 524288
  117.7 1.7 %copy.22 = f32[256,256]{1,0:T(8,128)} copy(f32[256,256]{1,0:T(8,128)} %get-tuple-element.23) | data formatting | bytes 524288
  (1 shorter events, 0.0 us)

commit v2 on v0

v2 whole, which is shorter than its diff:
```python
import jax
import jax.numpy as jnp
from jax import lax
from jax.experimental import pallas as pl
from jax.experimental.pallas import tpu as pltpu
from jax.sharding import PartitionSpec as P

MESH = pl.DeviceIdType.MESH
BF = jnp.bfloat16
F32 = jnp.float32
SLOTS = 96
ZERO = SLOTS
TN = (((0,), (0,)), ((), ()))
NT = (((1,), (1,)), ((), ()))


def mod4(v):
    return lax.rem(v, 4)


def xor4(v, d):
    v0, v1, d0, d1 = lax.rem(v, 2), lax.div(v, 2), d % 2, d // 2
    return 2 * (v1 + d1 - 2 * v1 * d1) + v0 + d0 - 2 * v0 * d0


def z_far(n):
    return mod4(2 - n + 3 * lax.div(n * (n - 1), 2))


def z_near(n):
    return mod4(n + lax.div(n * (n - 1), 2))


def dot(a, b):
    return jnp.dot(a, b, preferred_element_type=F32)


def kernel(
    rows_in, cols_in, count_in, feat_h, tiles_h, w_self_h, w_neigh_h, bias, cot_h,
    out_h, gfeat_h, gself_h, gneigh_h, gbias_h,
    A, T, X, PA, CR, Y, YR, ZS, ZR, TOT, G, ACC, BP, XR, XS, LR,
    W, M, MC, M1, MX, M2, MY, M3, ML, M4, MH, R,
    w_self, w_neigh, cot, out, gfeat, gbias, table, inv,
    lsem, osem, s1z, r1z, s1x, r1x, s3c, r3c, s3y, r3y, s3z, r3z,
    s5z, r5z, s5y, r5y, s5c, r5c, s6x, r6x, s6l, r6l, sw, rw,
):
    i = lax.axis_index("row")
    j = lax.axis_index("col")
    zl, x = lax.div(i, 4), lax.rem(i, 4)
    zh, yc = lax.div(j, 8), lax.rem(j, 8)
    y, c = lax.div(yc, 2), lax.rem(yc, 2)
    oc = 1 - c

    def dev(zl_=zl, x_=x, zh_=zh, y_=y, c_=c):
        return (zl_ * 4 + x_, zh_ * 8 + y_ * 2 + c_)

    def to_x(d):
        return dev(x_=mod4(x + d))

    def to_y(d):
        return dev(y_=mod4(y + d))

    def to_zh(d):
        return dev(zh_=mod4(zh + d))

    def to_zl(d):
        return dev(zl_=xor4(zl, d))

    def remote(src, dst, ssem, rsem, device):
        return pltpu.make_async_remote_copy(
            src_ref=src, dst_ref=dst, send_sem=ssem, recv_sem=rsem, device_id=device, device_id_type=MESH
        )

    def each3(act):
        pl.loop(1, 4)(act)

    def z1(d):
        return remote(X.at[i], X.at[i], s1z.at[d - 1], r1z.at[d - 1], to_zl(d))

    def x1(d, e):
        block = X.at[xor4(zl, d) * 4 + x]
        return remote(block, block, s1x.at[d, e - 1], r1x.at[d, e - 1], to_x(e))

    def c3(n):
        return remote(PA.at[mod4(zh + z_far(n)), oc], CR.at[n], s3c.at[n], r3c.at[n], dev(c_=oc))

    def y3(n, d):
        share = Y.at[mod4(zh + z_far(n)), mod4(y + d)]
        return remote(share, YR.at[n, d - 1], s3y.at[n, d - 1], r3y.at[n, d - 1], to_y(d))

    def z3(n):
        return remote(ZS.at[n], ZR.at[n], s3z.at[n], r3z.at[n], to_zh(z_far(n)))

    def z5(d):
        return remote(G.at[zh, c, y], G.at[zh, c, y], s5z.at[d - 1], r5z.at[d - 1], to_zh(d))

    def y5(g, d):
        block = G.at[mod4(zh + 4 - z_near(g)), c, y]
        return remote(block, block, s5y.at[g, d - 1], r5y.at[g, d - 1], to_y(d))

    def c5(g):
        slab = G.at[mod4(zh + 4 - z_near(g)), c]
        return remote(slab, slab, s5c.at[g], r5c.at[g], dev(c_=oc))

    def x6(n, d):
        share = BP.at[xor4(zl, 3 - n), mod4(x + d)]
        return remote(share, XR.at[n, d - 1], s6x.at[n, d - 1], r6x.at[n, d - 1], to_x(d))

    def l6(n):
        return remote(XS.at[n], LR.at[n], s6l.at[n], r6l.at[n], to_zl(3 - n))

    def w(k, src, dst, device):
        return remote(src, dst, sw.at[k], rw.at[k], device)

    def wc():
        return w(0, M.at[oc], MC, dev(c_=oc))

    def wx(d):
        return w(d, M1.at[mod4(x + d)], MX.at[d - 1], to_x(d))

    def wy(d):
        return w(3 + d, M2.at[mod4(y + d)], MY.at[d - 1], to_y(d))

    def wl(d):
        return w(6 + d, M3, ML.at[d - 1], to_zl(d))

    def wh(d):
        return w(9 + d, M4, MH.at[d - 1], to_zh(d))

    def vy(d):
        return w(12 + d, R.at[c, x, y], R.at[c, x, y], to_y(d))

    def vx(d):
        return w(15 + d, R.at[c, x], R.at[c, x], to_x(d))

    def vc():
        return w(19, R.at[c], R.at[c], dev(c_=oc))

    barrier = pltpu.get_barrier_semaphore()

    def greet(device):
        pl.semaphore_signal(barrier, inc=1, device_id=device, device_id_type=MESH)

    @each3
    def _(d):
        greet(to_zh(d))
        greet(to_zl(d))
        greet(to_x(d))
        greet(to_y(d))

    greet(dev(c_=oc))

    loads = [
        pltpu.make_async_copy(feat_h, X.at[i], lsem.at[0]),
        pltpu.make_async_copy(tiles_h.at[0, 0], T.at[pl.ds(0, SLOTS)], lsem.at[1]),
        pltpu.make_async_copy(w_self_h, w_self, lsem.at[2]),
        pltpu.make_async_copy(w_neigh_h, w_neigh, lsem.at[3]),
        pltpu.make_async_copy(cot_h, cot, lsem.at[4]),
    ]
    for load in loads:
        load.start()

    place_id = lax.broadcasted_iota(jnp.int32, (8, 128), 0) * 128 + lax.broadcasted_iota(jnp.int32, (8, 128), 1)
    count = count_in[0, 0]

    def note(t, found):
        r = rows_in[0, 0, t]
        place = lax.div(r, 8) * 8 + lax.rem(r, 2) * 4 + lax.div(lax.rem(r, 8), 2)
        place = jnp.where(t < count, place * 16 + cols_in[0, 0, t], -1)
        return jnp.where(place_id == place, t, found)

    table[...] = lax.fori_loop(0, SLOTS, note, jnp.full((8, 128), ZERO, jnp.int32))
    to_smem = pltpu.make_async_copy(table, inv, lsem.at[5])
    to_smem.start()
    T[ZERO] = jnp.zeros((128, 128), BF)
    ACC[...] = jnp.zeros_like(ACC)
    loads[0].wait()
    pl.semaphore_wait(barrier, 13)

    each3(lambda d: z1(d).start())
    each3(lambda d: x1(0, d).start())
    to_smem.wait()
    for load in loads[1:]:
        load.wait()

    @pl.loop(0, 4)
    def _(d):
        @pl.when(d > 0)
        def _():
            z1(d).wait_recv()
            each3(lambda e: x1(d, e).start())

        @pl.loop(d * 8, d * 8 + 8)
        def _(p):
            tile_rows = pl.ds(pl.multiple_of(p * 128, 128), 128)
            for q in range(16):
                A[tile_rows, q * 128 : (q + 1) * 128] = T[inv[lax.div(p, 8), lax.rem(p, 8) * 16 + q]]

    own_term = dot(X[i], w_self[...]) + bias[...]

    @pl.loop(0, 4)
    def _(d):
        each3(lambda e: x1(d, e).wait_recv())

    @pl.loop(0, 5)
    def _(n):
        @pl.when(n < 4)
        def _():
            zq = mod4(zh + z_far(n))
            chunk = pl.ds(pl.multiple_of(zq * 1024, 1024), 1024)
            PA[zq] = dot(A[chunk, :], X[...].reshape(2048, 256)).astype(BF).reshape(2, 4, 128, 256)
            c3(n).start()

        @pl.when(n > 0)
        def _():
            zq = mod4(zh + z_far(n - 1))
            c3(n - 1).wait_recv()
            Y[zq] = (PA[zq, c].astype(F32) + CR[n - 1].astype(F32)).astype(BF)
            each3(lambda d: y3(n - 1, d).start())

    @pl.loop(0, 4)
    def _(n):
        each3(lambda d: y3(n, d).wait_recv())
        total = Y[mod4(zh + z_far(n)), y].astype(F32)
        for d in range(3):
            total = total + YR[n, d].astype(F32)
        TOT[...] = total

        @pl.when(n < 3)
        def _():
            ZS[n] = total.astype(BF)
            z3(n).start()

    total = TOT[...]
    for n in range(3):
        z3(n).wait_recv()
        total = total + ZR[n].astype(F32)
    aggregate = total.astype(BF)

    preact = own_term + dot(aggregate, w_neigh[...])
    sigma = jax.nn.sigmoid(preact)
    grad_pre = cot[...].astype(F32) * sigma * (1.0 + preact * (1.0 - sigma))
    grad_pre_b = grad_pre.astype(BF)
    G[zh, c, y] = lax.dot_general(grad_pre_b, w_neigh[...], NT, preferred_element_type=F32).astype(BF)

    z5(1).start()
    z5(3).start()
    z5(2).start()
    each3(lambda d: y5(0, d).start())
    out[...] = (preact * sigma).astype(BF)
    save_out = pltpu.make_async_copy(out, out_h, osem.at[0])
    save_out.start()

    W[0:256] = lax.dot_general(X[i], grad_pre_b, TN, preferred_element_type=F32)
    W[256:512] = lax.dot_general(aggregate, grad_pre_b, TN, preferred_element_type=F32)
    column = jnp.sum(grad_pre, axis=0, keepdims=True)
    row_id = lax.broadcasted_iota(jnp.int32, (8, 128), 0)
    bias_tile = jnp.where(row_id == 0, column[:, :128], jnp.where(row_id == 1, column[:, 128:], 0.0))

    @pl.loop(0, 32)
    def _(q):
        part = W[pl.ds(pl.multiple_of(q * 16, 16), 16), :]
        a, b = lax.div(q, 16), lax.rem(q, 16)
        u, v = lax.div(b, 4), lax.rem(b, 4)
        M[a, u, v, 0] = part[0:8, 0:128]
        M[a, u, v, 1] = part[0:8, 128:256]
        M[a, u, v, 2] = part[8:16, 0:128]
        M[a, u, v, 3] = part[8:16, 128:256]
        M[a, u, v, 4] = bias_tile

    wc().start()
    gfeat_own = lax.dot_general(grad_pre_b, w_self[...], NT, preferred_element_type=F32)
    wc().wait_recv()
    M1[...] = M[c] + MC[...]
    each3(lambda d: wx(d).start())

    @pl.loop(0, 4)
    def _(g):
        @pl.when(g < 3)
        def _():
            z5(z_near(g + 1)).wait_recv()
            each3(lambda d: y5(g + 1, d).start())

        each3(lambda d: y5(g, d).wait_recv())
        c5(g).start()

        @pl.when(g == 0)
        def _():
            each3(lambda d: wx(d).wait_recv())
            M2[...] = M1[x] + MX[0] + MX[1] + MX[2]
            each3(lambda d: wy(d).start())

        @pl.when(g == 1)
        def _():
            each3(lambda d: wy(d).wait_recv())
            M3[...] = M2[y] + MY[0] + MY[1] + MY[2]
            each3(lambda d: wl(d).start())

        @pl.when(g == 2)
        def _():
            each3(lambda d: wl(d).wait_recv())
            M4[...] = M3[...] + ML[0] + ML[1] + ML[2]
            each3(lambda d: wh(d).start())

        c5(g).wait_recv()
        zq = mod4(zh + 4 - z_near(g))
        chunk = pl.ds(pl.multiple_of(zq * 1024, 1024), 1024)

        @pl.loop(0, 4)
        def _(n):
            part = xor4(zl, 3 - n)
            columns = pl.ds(pl.multiple_of(part * 512, 512), 512)
            ACC[part] += lax.dot_general(
                A[chunk, columns], G[zq].reshape(1024, 256), TN, preferred_element_type=F32
            )

            @pl.when(g == 3)
            def _():
                BP[part] = ACC[part].astype(BF).reshape(4, 128, 256)
                each3(lambda d: x6(n, d).start())

    each3(lambda d: wh(d).wait_recv())
    sums = M4[...] + (MH[0] + MH[1] + MH[2])
    R[c, x, y] = sums[0:4]
    each3(lambda d: vy(d).start())

    @pl.loop(0, 4)
    def _(n):
        each3(lambda d: x6(n, d).wait_recv())
        part_sum = BP[xor4(zl, 3 - n), x].astype(F32)
        for d in range(3):
            part_sum = part_sum + XR[n, d].astype(F32)
        TOT[...] = part_sum

        @pl.when(n < 3)
        def _():
            XS[n] = part_sum.astype(BF)
            l6(n).start()

        @pl.when(n == 1)
        def _():
            each3(lambda d: vy(d).wait_recv())
            each3(lambda d: vx(d).start())

    factor = 1.0 / 256.0
    gbias[...] = jnp.concatenate([sums[4, 0:1], sums[4, 1:2]], axis=1) * factor
    each3(lambda d: vx(d).wait_recv())
    vc().start()
    total = TOT[...] + gfeat_own
    for n in range(3):
        l6(n).wait_recv()
        total = total + LR[n].astype(F32)
    gfeat[...] = total.astype(BF)
    vc().wait_recv()

    @pl.loop(0, 32)
    def _(q):
        a, b = lax.div(q, 16), lax.rem(q, 16)
        u, v = lax.div(b, 4), lax.rem(b, 4)
        upper = jnp.concatenate([R[a, u, v, 0], R[a, u, v, 1]], axis=1)
        lower = jnp.concatenate([R[a, u, v, 2], R[a, u, v, 3]], axis=1)
        W[pl.ds(pl.multiple_of(q * 16, 16), 16), :] = jnp.concatenate([upper, lower], axis=0) * factor

    saves = [
        pltpu.make_async_copy(gfeat, gfeat_h, osem.at[1]),
        pltpu.make_async_copy(W.at[pl.ds(0, 256)], gself_h, osem.at[2]),
        pltpu.make_async_copy(W.at[pl.ds(256, 256)], gneigh_h, osem.at[3]),
        pltpu.make_async_copy(gbias, gbias_h, osem.at[4]),
    ]
    for save in saves:
        save.start()

    @pl.loop(0, 4)
    def _(n):
        c3(n).wait_send()
        c5(n).wait_send()

        @each3
        def _(d):
            x1(n, d).wait_send()
            y3(n, d).wait_send()
            y5(n, d).wait_send()
            x6(n, d).wait_send()

    @each3
    def _(d):
        for copy in (z1(d), z3(d - 1), z5(d), l6(d - 1), wx(d), wy(d), wl(d), wh(d), vy(d), vx(d)):
            copy.wait_send()

    wc().wait_send()
    vc().wait_send()
    save_out.wait()
    for save in saves:
        save.wait()


def hand_over(*refs):
    n = len(refs) // 2
    for k in range(n):
        refs[n + k][...] = refs[k][...]


def body(features, adj_tiles, tile_row, tile_col, tile_count, w_self, w_neigh, bias_vec, cotangent):
    smem = pl.BlockSpec(memory_space=pltpu.SMEM)
    vmem = pl.BlockSpec(memory_space=pltpu.VMEM)
    whole = pl.BlockSpec(memory_space=pl.ANY)
    dma = pltpu.SemaphoreType.DMA
    sds = jax.ShapeDtypeStruct
    results = (
        sds((128, 256), BF), sds((128, 256), BF), sds((256, 256), F32), sds((256, 256), F32), sds((1, 256), F32),
    )
    held = pl.pallas_call(
        kernel,
        out_shape=results,
        in_specs=[smem, smem, smem, whole, whole, whole, whole, vmem, whole],
        out_specs=(whole,) * 5,
        scratch_shapes=[
            pltpu.VMEM((4096, 2048), BF),
            pltpu.VMEM((SLOTS + 1, 128, 128), BF),
            pltpu.VMEM((16, 128, 256), BF),
            pltpu.VMEM((4, 2, 4, 128, 256), BF),
            pltpu.VMEM((4, 4, 128, 256), BF),
            pltpu.VMEM((4, 4, 128, 256), BF),
            pltpu.VMEM((4, 3, 128, 256), BF),
            pltpu.VMEM((3, 128, 256), BF),
            pltpu.VMEM((3, 128, 256), BF),
            pltpu.VMEM((128, 256), F32),
            pltpu.VMEM((4, 2, 4, 128, 256), BF),
            pltpu.VMEM((4, 512, 256), F32),
            pltpu.VMEM((4, 4, 128, 256), BF),
            pltpu.VMEM((4, 3, 128, 256), BF),
            pltpu.VMEM((3, 128, 256), BF),
            pltpu.VMEM((3, 128, 256), BF),
            pltpu.VMEM((512, 256), F32),
            pltpu.VMEM((2, 4, 4, 5, 8, 128), F32),
            pltpu.VMEM((4, 4, 5, 8, 128), F32),
            pltpu.VMEM((4, 4, 5, 8, 128), F32),
            pltpu.VMEM((3, 4, 5, 8, 128), F32),
            pltpu.VMEM((4, 5, 8, 128), F32),
            pltpu.VMEM((3, 5, 8, 128), F32),
            pltpu.VMEM((5, 8, 128), F32),
            pltpu.VMEM((3, 5, 8, 128), F32),
            pltpu.VMEM((5, 8, 128), F32),
            pltpu.VMEM((3, 5, 8, 128), F32),
            pltpu.VMEM((2, 4, 4, 4, 8, 128), F32),
            pltpu.VMEM((256, 256), BF),
            pltpu.VMEM((256, 256), BF),
            pltpu.VMEM((128, 256), BF),
            pltpu.VMEM((128, 256), BF),
            pltpu.VMEM((128, 256), BF),
            pltpu.VMEM((1, 256), F32),
            pltpu.VMEM((8, 128), jnp.int32),
            pltpu.SMEM((8, 128), jnp.int32),
            dma((6,)), dma((5,)),
            dma((3,)), dma((3,)), dma((4, 3)), dma((4, 3)),
            dma((4,)), dma((4,)), dma((4, 3)), dma((4, 3)), dma((3,)), dma((3,)),
            dma((3,)), dma((3,)), dma((4, 3)), dma((4, 3)), dma((4,)), dma((4,)),
            dma((4, 3)), dma((4, 3)), dma((3,)), dma((3,)),
            dma((20,)), dma((20,)),
        ],
        compiler_params=pltpu.CompilerParams(
            collective_id=0, has_side_effects=True, vmem_limit_bytes=60 * 2**20
        ),
    )(
        tile_row, tile_col, tile_count, features, adj_tiles, w_self, w_neigh, bias_vec.reshape(1, 256), cotangent
    )
    out, gfeat, gself, gneigh, gbias = pl.pallas_call(
        hand_over,
        out_shape=results,
        in_specs=[vmem] * 5,
        out_specs=(vmem,) * 5,
    )(*held)
    return out, gfeat, gself, gneigh, gbias.reshape(256)


def solution(mesh):
    placed = (
        P(("row", "col"), None),
        P("row", "col", None, None, None),
        P("row", "col", None),
        P("row", "col", None),
        P("row", "col"),
        P(),
        P(),
        P(),
        P(("row", "col"), None),
    )
    return jax.shard_map(
        body,
        mesh=mesh,
        in_specs=placed,
        out_specs=(P(("row", "col"), None), P(("row", "col"), None), P(), P(), P()),
        check_vma=False,
    )
```

time: 921 us -> 108 us (0.12); the launches traced: 910 us -> 108 us
  waiting for transfers between devices: 650 us -> 0 us
  Pallas kernels: 0 us -> 107 us
  blocking collectives: 103 us -> 0 us
  other arithmetic: 66.8 us -> 0 us
  local copies, waits for them, and re-layouts: 46.5 us -> 0 us
  matrix products: 28.5 us -> 0 us
  between operations: 14.6 us -> 1.29 us
    psum x1 -> x0, waiting for transfers between devices: 293 us -> none  [body(): lax.psum((self_term, neigh_term, bias_term), ('row', 'col'))]
    reduce_scatter x2 -> x0, waiting for transfers between devices: 204 us -> none  [the longest x1 129 us: body(): lax.psum_scatter(partial_rows.astype(jnp.bfloat16), 'col', scatter_dimens...]
    all_gather x2 -> x0, waiting for transfers between devices: 153 us -> none  [the longest x1 81.6 us: body(): column_block = lax.all_gather(features, 'row', axis=0, tiled=True)]
    pallas_call x0 -> x2, Pallas kernels: none -> 107 us  [the longest x1 105 us: body(): pl.pallas_call(kernel, out_shape=results, in_specs=[smem, smem, smem, who...]
    psum x1 -> x0, blocking collectives: 103 us -> none  [body(): lax.psum((self_term, neigh_term, bias_term), ('row', 'col'))]
    scatter-add x2 -> x0, other arithmetic: 56.6 us -> none  [place_tiles(): placed = jnp.zeros((segments, products.shape[1], products.shape[2]), jnp....]
    dot_general x8 -> x0, matrix products: 28.5 us -> none  [the longest x1 9.85 us: slot_products(): jnp.einsum('tab,tbf->taf', tile_values, picked, preferred_element_type=jn...]
    mul x2 -> x0, local copies, waits for them, and re-layouts: 25.2 us -> none  [place_tiles(): weighted = products * occupied[:, None, None]]
  transfers between devices with their start and end apart: 5 -> 0, of which waited for: 5 -> 0; matrix products, arithmetic and copies ran while one was open for 8% -> 0% of each run, Pallas kernels for 0% -> 0%
where the time goes in v2:
time: 108 us
  Pallas kernels  107 us (99%)
  between operations  1.29 us (1%)
    pallas_call x1, Pallas kernels, body(): pl.pallas_call(kernel, out_shape=results, in_specs=[smem, smem, smem, who...  105 us

profile of v2, /device:TPU:1, one launch (start us, length us, event | category | flops | bytes accessed | tf_op | source)
XLA Modules:
  0.0 108.0 jit_solution(16923309516517975885)
XLA Ops:
  1.3 104.8 %shard_map.128 = (bf16[128,256]{1,0:T(8,128)(2,1)}, bf16[128,256]{1,0:T(8,128)(2,1)}, f32[256,256]{1,0:T(8,128)}, f32[256,256]{1,0:T(8,128)}, f32[1,256]{1,0:T(1,128)}) custom-call(s32[1,1,96]{2,1,0:T(1,128)} %rows_in.1, s32[1,1,96]{2,1,0:T(1,128)} %cols_in.1, s32[1,1]{1,0:T(1,128)S(6)} %copy.14.count_in, bf16[128,256]{1,0:T(8,128)(2,1)} %feat_h.1, ...), custom_call_target="tpu_custom_call" | custom-call | tf_op jit(solution)/shard_map/pallas_call | solution.py:412
  106.1 1.9 %shard_map.129 = (bf16[128,256]{1,0:T(8,128)(2,1)}, bf16[128,256]{1,0:T(8,128)(2,1)}, f32[256,256]{1,0:T(8,128)}, f32[256,256]{1,0:T(8,128)}, f32[1,256]{1,0:T(1,128)}) custom-call(bf16[128,256]{1,0:T(8,128)(2,1)} %get-tuple-element.15.refs_0_, bf16[128,256]{1,0:T(8,128)(2,1)} %get-tuple-element.16.refs_1_, f32[256,256]{1,0:T(8,128)} %get-tuple-element.17.refs_2_, ...), custom_call_target="tpu_custom_call" | custom-call | tf_op jit(solution)/shard_map/pallas_call | solution.py:467

commit v3 on v2

--- a/solution.py
+++ b/solution.py
@@ -36,11 +36,11 @@
 
 
 def kernel(
-    rows_in, cols_in, count_in, feat_h, tiles_h, w_self_h, w_neigh_h, bias, cot_h,
+    rows_h, cols_h, count_h, feat_h, tiles_h, w_self_h, w_neigh_h, bias_h, cot_h,
     out_h, gfeat_h, gself_h, gneigh_h, gbias_h,
     A, T, X, PA, CR, Y, YR, ZS, ZR, TOT, G, ACC, BP, XR, XS, LR,
     W, M, MC, M1, MX, M2, MY, M3, ML, M4, MH, R,
-    w_self, w_neigh, cot, out, gfeat, gbias, table, inv,
+    w_self, w_neigh, bias, cot, out, gfeat, gbias, rows_in, cols_in, count_in, table, inv,
     lsem, osem, s1z, r1z, s1x, r1x, s3c, r3c, s3y, r3y, s3z, r3z,
     s5z, r5z, s5y, r5y, s5c, r5c, s6x, r6x, s6l, r6l, sw, rw,
 ):
@@ -88,11 +88,20 @@
         share = Y.at[mod4(zh + z_far(n)), mod4(y + d)]
         return remote(share, YR.at[n, d - 1], s3y.at[n, d - 1], r3y.at[n, d - 1], to_y(d))
 
+    def half(ref, k):
+        return ref.at[pl.ds(64 * k, 64)]
+
     def z3(n):
-        return remote(ZS.at[n], ZR.at[n], s3z.at[n], r3z.at[n], to_zh(z_far(n)))
-
-    def z5(d):
-        return remote(G.at[zh, c, y], G.at[zh, c, y], s5z.at[d - 1], r5z.at[d - 1], to_zh(d))
+        src = half(ZS.at[0], n) if n < 2 else ZS.at[n - 1]
+        dst = half(ZR.at[0], n) if n < 2 else ZR.at[n - 1]
+        return remote(src, dst, s3z.at[n], r3z.at[n], to_zh(1 + 2 * (n % 2)))
+
+    def z5(k):
+        if k < 2:
+            block = G.at[zh, c, y]
+        else:
+            block = half(G.at[mod4(zh + 3 - 2 * (k % 2)), c, y], k % 2)
+        return remote(block, block, s5z.at[k], r5z.at[k], to_zh(1 + 2 * (k % 2)))
 
     def y5(g, d):
         block = G.at[mod4(zh + 4 - z_near(g)), c, y]
@@ -124,14 +133,14 @@
     def wl(d):
         return w(6 + d, M3, ML.at[d - 1], to_zl(d))
 
-    def wh(d):
-        return w(9 + d, M4, MH.at[d - 1], to_zh(d))
+    def wh(k):
+        return w(20 if k == 2 else 10 + k, MH.at[0] if k == 2 else M4, MH.at[k], to_zh(1 + 2 * (k % 2)))
+
+    def vx(d):
+        return w(12 + d, R.at[c, y, x], R.at[c, y, x], to_x(d))
 
     def vy(d):
-        return w(12 + d, R.at[c, x, y], R.at[c, x, y], to_y(d))
-
-    def vx(d):
-        return w(15 + d, R.at[c, x], R.at[c, x], to_x(d))
+        return w(15 + d, R.at[c, y], R.at[c, y], to_y(d))
 
     def vc():
         return w(19, R.at[c], R.at[c], dev(c_=oc))
@@ -143,12 +152,13 @@
 
     @each3
     def _(d):
-        greet(to_zh(d))
         greet(to_zl(d))
         greet(to_x(d))
         greet(to_y(d))
 
     greet(dev(c_=oc))
+    greet(to_zh(1))
+    greet(to_zh(3))
 
     loads = [
         pltpu.make_async_copy(feat_h, X.at[i], lsem.at[0]),
@@ -156,10 +166,16 @@
         pltpu.make_async_copy(w_self_h, w_self, lsem.at[2]),
         pltpu.make_async_copy(w_neigh_h, w_neigh, lsem.at[3]),
         pltpu.make_async_copy(cot_h, cot, lsem.at[4]),
+        pltpu.make_async_copy(bias_h, bias, lsem.at[5]),
+        pltpu.make_async_copy(rows_h, rows_in, lsem.at[6]),
+        pltpu.make_async_copy(cols_h, cols_in, lsem.at[7]),
+        pltpu.make_async_copy(count_h, count_in, lsem.at[8]),
     ]
     for load in loads:
         load.start()
 
+    for load in loads[6:]:
+        load.wait()
     place_id = lax.broadcasted_iota(jnp.int32, (8, 128), 0) * 128 + lax.broadcasted_iota(jnp.int32, (8, 128), 1)
     count = count_in[0, 0]
 
@@ -170,17 +186,17 @@
         return jnp.where(place_id == place, t, found)
 
     table[...] = lax.fori_loop(0, SLOTS, note, jnp.full((8, 128), ZERO, jnp.int32))
-    to_smem = pltpu.make_async_copy(table, inv, lsem.at[5])
+    to_smem = pltpu.make_async_copy(table, inv, lsem.at[9])
     to_smem.start()
     T[ZERO] = jnp.zeros((128, 128), BF)
     ACC[...] = jnp.zeros_like(ACC)
     loads[0].wait()
-    pl.semaphore_wait(barrier, 13)
+    pl.semaphore_wait(barrier, 12)
 
     each3(lambda d: z1(d).start())
     each3(lambda d: x1(0, d).start())
     to_smem.wait()
-    for load in loads[1:]:
+    for load in loads[1:6]:
         load.wait()
 
     @pl.loop(0, 4)
@@ -226,15 +242,25 @@
             total = total + YR[n, d].astype(F32)
         TOT[...] = total
 
-        @pl.when(n < 3)
-        def _():
-            ZS[n] = total.astype(BF)
-            z3(n).start()
-
-    total = TOT[...]
-    for n in range(3):
-        z3(n).wait_recv()
-        total = total + ZR[n].astype(F32)
+        @pl.when(n == 0)
+        def _():
+            ZS[0] = total.astype(BF)
+            z3(0).start()
+            z3(1).start()
+
+        for k in range(2):
+
+            @pl.when(n == 1 + k)
+            def _():
+                z3(k).wait_recv()
+                near = slice(64 * k, 64 * k + 64)
+                TOT[near] += ZR[0, near].astype(F32)
+                ZS[1 + k] = TOT[...].astype(BF)
+                z3(2 + k).start()
+
+    z3(2).wait_recv()
+    z3(3).wait_recv()
+    total = TOT[...] + ZR[1].astype(F32) + ZR[2].astype(F32)
     aggregate = total.astype(BF)
 
     preact = own_term + dot(aggregate, w_neigh[...])
@@ -243,9 +269,8 @@
     grad_pre_b = grad_pre.astype(BF)
     G[zh, c, y] = lax.dot_general(grad_pre_b, w_neigh[...], NT, preferred_element_type=F32).astype(BF)
 
+    z5(0).start()
     z5(1).start()
-    z5(3).start()
-    z5(2).start()
     each3(lambda d: y5(0, d).start())
     out[...] = (preact * sigma).astype(BF)
     save_out = pltpu.make_async_copy(out, out_h, osem.at[0])
@@ -274,21 +299,27 @@
     M1[...] = M[c] + MC[...]
     each3(lambda d: wx(d).start())
 
+    each3(lambda d: wx(d).wait_recv())
+    M2[...] = M1[x] + MX[0] + MX[1] + MX[2]
+    each3(lambda d: wy(d).start())
+
     @pl.loop(0, 4)
     def _(g):
+        for k in range(2):
+
+            @pl.when(g == k)
+            def _():
+                z5(k).wait_recv()
+                z5(2 + k).start()
+
+        @pl.when(g == 2)
+        def _():
+            z5(2).wait_recv()
+            z5(3).wait_recv()
+
         @pl.when(g < 3)
         def _():
-            z5(z_near(g + 1)).wait_recv()
             each3(lambda d: y5(g + 1, d).start())
-
-        each3(lambda d: y5(g, d).wait_recv())
-        c5(g).start()
-
-        @pl.when(g == 0)
-        def _():
-            each3(lambda d: wx(d).wait_recv())
-            M2[...] = M1[x] + MX[0] + MX[1] + MX[2]
-            each3(lambda d: wy(d).start())
 
         @pl.when(g == 1)
         def _():
@@ -299,9 +330,17 @@
         @pl.when(g == 2)
         def _():
             each3(lambda d: wl(d).wait_recv())
-            M4[...] = M3[...] + ML[0] + ML[1] + ML[2]
-            each3(lambda d: wh(d).start())
-
+            M4[...] = (M3[...] + ML[0]) + (ML[1] + ML[2])
+            wh(0).start()
+            wh(1).start()
+
+        @pl.when(g == 3)
+        def _():
+            wh(0).wait_recv()
+            wh(2).start()
+
+        each3(lambda d: y5(g, d).wait_recv())
+        c5(g).start()
         c5(g).wait_recv()
         zq = mod4(zh + 4 - z_near(g))
         chunk = pl.ds(pl.multiple_of(zq * 1024, 1024), 1024)
@@ -317,12 +356,18 @@
             @pl.when(g == 3)
             def _():
                 BP[part] = ACC[part].astype(BF).reshape(4, 128, 256)
+
+            @pl.when((g == 3) & (n < 2))
+            def _():
                 each3(lambda d: x6(n, d).start())
 
-    each3(lambda d: wh(d).wait_recv())
-    sums = M4[...] + (MH[0] + MH[1] + MH[2])
-    R[c, x, y] = sums[0:4]
-    each3(lambda d: vy(d).start())
+    wh(1).wait_recv()
+    wh(2).wait_recv()
+    sums = (M4[...] + MH[2]) + (MH[0] + MH[1])
+    R[c, y, x] = sums[0:4]
+    each3(lambda d: vx(d).start())
+    each3(lambda d: x6(2, d).start())
+    each3(lambda d: x6(3, d).start())
 
     @pl.loop(0, 4)
     def _(n):
@@ -339,28 +384,31 @@
 
         @pl.when(n == 1)
         def _():
-            each3(lambda d: vy(d).wait_recv())
-            each3(lambda d: vx(d).start())
+            each3(lambda d: vx(d).wait_recv())
+            each3(lambda d: vy(d).start())
 
     factor = 1.0 / 256.0
     gbias[...] = jnp.concatenate([sums[4, 0:1], sums[4, 1:2]], axis=1) * factor
-    each3(lambda d: vx(d).wait_recv())
+    each3(lambda d: vy(d).wait_recv())
     vc().start()
+
+    def assemble(a):
+        @pl.loop(0, 16)
+        def _(q):
+            u, v = lax.div(q, 4), lax.rem(q, 4)
+            upper = jnp.concatenate([R[a, v, u, 0], R[a, v, u, 1]], axis=1)
+            lower = jnp.concatenate([R[a, v, u, 2], R[a, v, u, 3]], axis=1)
+            rows = pl.ds(pl.multiple_of(a * 256 + q * 16, 16), 16)
+            W[rows, :] = jnp.concatenate([upper, lower], axis=0) * factor
+
+    assemble(c)
     total = TOT[...] + gfeat_own
     for n in range(3):
         l6(n).wait_recv()
         total = total + LR[n].astype(F32)
     gfeat[...] = total.astype(BF)
     vc().wait_recv()
-
-    @pl.loop(0, 32)
-    def _(q):
-        a, b = lax.div(q, 16), lax.rem(q, 16)
-        u, v = lax.div(b, 4), lax.rem(b, 4)
-        upper = jnp.concatenate([R[a, u, v, 0], R[a, u, v, 1]], axis=1)
-        lower = jnp.concatenate([R[a, u, v, 2], R[a, u, v, 3]], axis=1)
-        W[pl.ds(pl.multiple_of(q * 16, 16), 16), :] = jnp.concatenate([upper, lower], axis=0) * factor
-
+    assemble(oc)
     saves = [
         pltpu.make_async_copy(gfeat, gfeat_h, osem.at[1]),
         pltpu.make_async_copy(W.at[pl.ds(0, 256)], gself_h, osem.at[2]),
@@ -384,11 +432,11 @@
 
     @each3
     def _(d):
-        for copy in (z1(d), z3(d - 1), z5(d), l6(d - 1), wx(d), wy(d), wl(d), wh(d), vy(d), vx(d)):
+        for copy in (z1(d), l6(d - 1), wx(d), wy(d), wl(d), vy(d), vx(d)):
             copy.wait_send()
 
-    wc().wait_send()
-    vc().wait_send()
+    for copy in (wc(), vc(), wh(0), wh(1), wh(2), *map(z3, range(4)), *map(z5, range(4))):
+        copy.wait_send()
     save_out.wait()
     for save in saves:
         save.wait()
@@ -401,7 +449,6 @@
 
 
 def body(features, adj_tiles, tile_row, tile_col, tile_count, w_self, w_neigh, bias_vec, cotangent):
-    smem = pl.BlockSpec(memory_space=pltpu.SMEM)
     vmem = pl.BlockSpec(memory_space=pltpu.VMEM)
     whole = pl.BlockSpec(memory_space=pl.ANY)
     dma = pltpu.SemaphoreType.DMA
@@ -412,7 +459,7 @@
     held = pl.pallas_call(
         kernel,
         out_shape=results,
-        in_specs=[smem, smem, smem, whole, whole, whole, whole, vmem, whole],
+        in_specs=[whole] * 9,
         out_specs=(whole,) * 5,
         scratch_shapes=[
             pltpu.VMEM((4096, 2048), BF),
@@ -445,18 +492,22 @@
             pltpu.VMEM((2, 4, 4, 4, 8, 128), F32),
             pltpu.VMEM((256, 256), BF),
             pltpu.VMEM((256, 256), BF),
+            pltpu.VMEM((1, 256), F32),
             pltpu.VMEM((128, 256), BF),
             pltpu.VMEM((128, 256), BF),
             pltpu.VMEM((128, 256), BF),
             pltpu.VMEM((1, 256), F32),
+            pltpu.SMEM((1, 1, SLOTS), jnp.int32),
+            pltpu.SMEM((1, 1, SLOTS), jnp.int32),
+            pltpu.SMEM((1, 1), jnp.int32),
             pltpu.VMEM((8, 128), jnp.int32),
             pltpu.SMEM((8, 128), jnp.int32),
-            dma((6,)), dma((5,)),
+            dma((10,)), dma((5,)),
             dma((3,)), dma((3,)), dma((4, 3)), dma((4, 3)),
-            dma((4,)), dma((4,)), dma((4, 3)), dma((4, 3)), dma((3,)), dma((3,)),
-            dma((3,)), dma((3,)), dma((4, 3)), dma((4, 3)), dma((4,)), dma((4,)),
+            dma((4,)), dma((4,)), dma((4, 3)), dma((4, 3)), dma((4,)), dma((4,)),
+            dma((4,)), dma((4,)), dma((4, 3)), dma((4, 3)), dma((4,)), dma((4,)),
             dma((4, 3)), dma((4, 3)), dma((3,)), dma((3,)),
-            dma((20,)), dma((20,)),
+            dma((21,)), dma((21,)),
         ],
         compiler_params=pltpu.CompilerParams(
             collective_id=0, has_side_effects=True, vmem_limit_bytes=60 * 2**20

time: 108 us -> 101 us (0.935)
  Pallas kernels: 107 us -> 99.9 us
    pallas_call x1, Pallas kernels: 105 us -> 98 us  [body(): pl.pallas_call(kernel, out_shape=results, in_specs=[whole] * 9, out_specs...]
where the time goes in v3:
time: 101 us
  Pallas kernels  99.9 us (99%)
  between operations  1.29 us (1%)
    pallas_call x1, Pallas kernels, body(): pl.pallas_call(kernel, out_shape=results, in_specs=[whole] * 9, out_specs...  98 us

profile of v3, /device:TPU:1, one launch (start us, length us, event | category | flops | bytes accessed | tf_op | source)
XLA Modules:
  0.0 101.2 jit_solution(16883013207648141792)
XLA Ops:
  1.3 98.0 %shard_map.128 = (bf16[128,256]{1,0:T(8,128)(2,1)}, bf16[128,256]{1,0:T(8,128)(2,1)}, f32[256,256]{1,0:T(8,128)}, f32[256,256]{1,0:T(8,128)}, f32[1,256]{1,0:T(1,128)}) custom-call(s32[1,1,96]{2,1,0:T(1,128)} %rows_h.1, s32[1,1,96]{2,1,0:T(1,128)} %cols_h.1, s32[1,1]{1,0:T(1,128)S(6)} %copy.14.count_h, bf16[128,256]{1,0:T(8,128)(2,1)} %feat_h.1, ...), custom_call_target="tpu_custom_call" | custom-call | tf_op jit(solution)/shard_map/pallas_call | solution.py:459
  99.3 1.9 %shard_map.129 = (bf16[128,256]{1,0:T(8,128)(2,1)}, bf16[128,256]{1,0:T(8,128)(2,1)}, f32[256,256]{1,0:T(8,128)}, f32[256,256]{1,0:T(8,128)}, f32[1,256]{1,0:T(1,128)}) custom-call(bf16[128,256]{1,0:T(8,128)(2,1)} %get-tuple-element.15.refs_0_, bf16[128,256]{1,0:T(8,128)(2,1)} %get-tuple-element.16.refs_1_, f32[256,256]{1,0:T(8,128)} %get-tuple-element.17.refs_2_, ...), custom_call_target="tpu_custom_call" | custom-call | tf_op jit(solution)/shard_map/pallas_call | solution.py:518

commit v4 on v3

--- a/solution.py
+++ b/solution.py
@@ -72,7 +72,7 @@
         )
 
     def each3(act):
-        pl.loop(1, 4)(act)
+        pl.loop(1, 4)(lambda k: act(1 + lax.rem(k, 3)))
 
     def z1(d):
         return remote(X.at[i], X.at[i], s1z.at[d - 1], r1z.at[d - 1], to_zl(d))
@@ -193,20 +193,20 @@
     loads[0].wait()
     pl.semaphore_wait(barrier, 12)
 
-    each3(lambda d: z1(d).start())
+    pl.loop(0, 3)(lambda k: z1(3 - k).start())
     each3(lambda d: x1(0, d).start())
     to_smem.wait()
     for load in loads[1:6]:
         load.wait()
 
     @pl.loop(0, 4)
-    def _(d):
-        @pl.when(d > 0)
-        def _():
-            z1(d).wait_recv()
-            each3(lambda e: x1(d, e).start())
-
-        @pl.loop(d * 8, d * 8 + 8)
+    def _(n):
+        @pl.when(n > 0)
+        def _():
+            z1(4 - n).wait_recv()
+            each3(lambda e: x1(4 - n, e).start())
+
+        @pl.loop(n * 8, n * 8 + 8)
         def _(p):
             tile_rows = pl.ds(pl.multiple_of(p * 128, 128), 128)
             for q in range(16):
@@ -276,31 +276,45 @@
     save_out = pltpu.make_async_copy(out, out_h, osem.at[0])
     save_out.start()
 
+    def split(value):
+        high = value.astype(BF).astype(F32)
+        return jnp.concatenate([high, value - high], axis=0).astype(BF)
+
+    def joined(tile):
+        return tile[0:8] + tile[8:16]
+
+    def keep(ref, total):
+        ref[...] = total.astype(BF)
+        lead = total.ndim - 3
+        tile = split(joined(total[(0,) * lead + (2,)]))
+        ref[(slice(None),) * lead + (2,)] = jnp.broadcast_to(tile, total.shape[:lead] + tile.shape)
+
+    def wide(value):
+        return value.astype(F32)
+
     W[0:256] = lax.dot_general(X[i], grad_pre_b, TN, preferred_element_type=F32)
     W[256:512] = lax.dot_general(aggregate, grad_pre_b, TN, preferred_element_type=F32)
     column = jnp.sum(grad_pre, axis=0, keepdims=True)
     row_id = lax.broadcasted_iota(jnp.int32, (8, 128), 0)
-    bias_tile = jnp.where(row_id == 0, column[:, :128], jnp.where(row_id == 1, column[:, 128:], 0.0))
+    bias_tile = split(jnp.where(row_id == 0, column[:, :128], jnp.where(row_id == 1, column[:, 128:], 0.0)))
 
     @pl.loop(0, 32)
     def _(q):
-        part = W[pl.ds(pl.multiple_of(q * 16, 16), 16), :]
+        part = W[pl.ds(pl.multiple_of(q * 16, 16), 16), :].astype(BF)
         a, b = lax.div(q, 16), lax.rem(q, 16)
         u, v = lax.div(b, 4), lax.rem(b, 4)
-        M[a, u, v, 0] = part[0:8, 0:128]
-        M[a, u, v, 1] = part[0:8, 128:256]
-        M[a, u, v, 2] = part[8:16, 0:128]
-        M[a, u, v, 3] = part[8:16, 128:256]
-        M[a, u, v, 4] = bias_tile
+        M[a, u, v, 0] = part[:, 0:128]
+        M[a, u, v, 1] = part[:, 128:256]
+        M[a, u, v, 2] = bias_tile
 
     wc().start()
     gfeat_own = lax.dot_general(grad_pre_b, w_self[...], NT, preferred_element_type=F32)
     wc().wait_recv()
-    M1[...] = M[c] + MC[...]
+    keep(M1, wide(M[c]) + wide(MC[...]))
     each3(lambda d: wx(d).start())
 
     each3(lambda d: wx(d).wait_recv())
-    M2[...] = M1[x] + MX[0] + MX[1] + MX[2]
+    keep(M2, wide(M1[x]) + wide(MX[0]) + wide(MX[1]) + wide(MX[2]))
     each3(lambda d: wy(d).start())
 
     @pl.loop(0, 4)
@@ -324,13 +338,13 @@
         @pl.when(g == 1)
         def _():
             each3(lambda d: wy(d).wait_recv())
-            M3[...] = M2[y] + MY[0] + MY[1] + MY[2]
+            keep(M3, wide(M2[y]) + wide(MY[0]) + wide(MY[1]) + wide(MY[2]))
             each3(lambda d: wl(d).start())
 
         @pl.when(g == 2)
         def _():
             each3(lambda d: wl(d).wait_recv())
-            M4[...] = (M3[...] + ML[0]) + (ML[1] + ML[2])
+            keep(M4, (wide(M3[...]) + wide(ML[0])) + (wide(ML[1]) + wide(ML[2])))
             wh(0).start()
             wh(1).start()
 
@@ -363,8 +377,8 @@
 
     wh(1).wait_recv()
     wh(2).wait_recv()
-    sums = (M4[...] + MH[2]) + (MH[0] + MH[1])
-    R[c, y, x] = sums[0:4]
+    sums = (wide(M4[...]) + wide(MH[2])) + (wide(MH[0]) + wide(MH[1]))
+    R[c, y, x] = sums[0:2].astype(BF)
     each3(lambda d: vx(d).start())
     each3(lambda d: x6(2, d).start())
     each3(lambda d: x6(3, d).start())
@@ -388,7 +402,8 @@
             each3(lambda d: vy(d).start())
 
     factor = 1.0 / 256.0
-    gbias[...] = jnp.concatenate([sums[4, 0:1], sums[4, 1:2]], axis=1) * factor
+    bias_sum = joined(sums[2])
+    gbias[...] = jnp.concatenate([bias_sum[0:1], bias_sum[1:2]], axis=1) * factor
     each3(lambda d: vy(d).wait_recv())
     vc().start()
 
@@ -396,10 +411,8 @@
         @pl.loop(0, 16)
         def _(q):
             u, v = lax.div(q, 4), lax.rem(q, 4)
-            upper = jnp.concatenate([R[a, v, u, 0], R[a, v, u, 1]], axis=1)
-            lower = jnp.concatenate([R[a, v, u, 2], R[a, v, u, 3]], axis=1)
             rows = pl.ds(pl.multiple_of(a * 256 + q * 16, 16), 16)
-            W[rows, :] = jnp.concatenate([upper, lower], axis=0) * factor
+            W[rows, :] = wide(jnp.concatenate([R[a, v, u, 0], R[a, v, u, 1]], axis=1)) * factor
 
     assemble(c)
     total = TOT[...] + gfeat_own
@@ -479,17 +492,17 @@
             pltpu.VMEM((3, 128, 256), BF),
             pltpu.VMEM((3, 128, 256), BF),
             pltpu.VMEM((512, 256), F32),
-            pltpu.VMEM((2, 4, 4, 5, 8, 128), F32),
-            pltpu.VMEM((4, 4, 5, 8, 128), F32),
-            pltpu.VMEM((4, 4, 5, 8, 128), F32),
-            pltpu.VMEM((3, 4, 5, 8, 128), F32),
-            pltpu.VMEM((4, 5, 8, 128), F32),
-            pltpu.VMEM((3, 5, 8, 128), F32),
-            pltpu.VMEM((5, 8, 128), F32),
-            pltpu.VMEM((3, 5, 8, 128), F32),
-            pltpu.VMEM((5, 8, 128), F32),
-            pltpu.VMEM((3, 5, 8, 128), F32),
-            pltpu.VMEM((2, 4, 4, 4, 8, 128), F32),
+            pltpu.VMEM((2, 4, 4, 3, 16, 128), BF),
+            pltpu.VMEM((4, 4, 3, 16, 128), BF),
+            pltpu.VMEM((4, 4, 3, 16, 128), BF),
+            pltpu.VMEM((3, 4, 3, 16, 128), BF),
+            pltpu.VMEM((4, 3, 16, 128), BF),
+            pltpu.VMEM((3, 3, 16, 128), BF),
+            pltpu.VMEM((3, 16, 128), BF),
+            pltpu.VMEM((3, 3, 16, 128), BF),
+            pltpu.VMEM((3, 16, 128), BF),
+            pltpu.VMEM((3, 3, 16, 128), BF),
+            pltpu.VMEM((2, 4, 4, 2, 16, 128), BF),
             pltpu.VMEM((256, 256), BF),
             pltpu.VMEM((256, 256), BF),
             pltpu.VMEM((1, 256), F32),

time: 101 us -> 97.2 us (0.962)
  Pallas kernels: 99.9 us -> 95.8 us
    pallas_call x1, Pallas kernels: 98 us -> 93.9 us  [body(): pl.pallas_call(kernel, out_shape=results, in_specs=[whole] * 9, out_specs...]
where the time goes in v4:
time: 97.2 us; the launch traced here: 97.1 us
  Pallas kernels  95.8 us (99%)
  between operations  1.29 us (1%)
    pallas_call x1, Pallas kernels, body(): pl.pallas_call(kernel, out_shape=results, in_specs=[whole] * 9, out_specs...  93.9 us

profile of v4, /device:TPU:1, one launch (start us, length us, event | category | flops | bytes accessed | tf_op | source)
XLA Modules:
  0.0 97.1 jit_solution(6958094404671689472)
XLA Ops:
  1.3 93.9 %shard_map.128 = (bf16[128,256]{1,0:T(8,128)(2,1)}, bf16[128,256]{1,0:T(8,128)(2,1)}, f32[256,256]{1,0:T(8,128)}, f32[256,256]{1,0:T(8,128)}, f32[1,256]{1,0:T(1,128)}) custom-call(s32[1,1,96]{2,1,0:T(1,128)} %rows_h.1, s32[1,1,96]{2,1,0:T(1,128)} %cols_h.1, s32[1,1]{1,0:T(1,128)S(6)} %copy.14.count_h, bf16[128,256]{1,0:T(8,128)(2,1)} %feat_h.1, ...), custom_call_target="tpu_custom_call" | custom-call | tf_op jit(solution)/shard_map/pallas_call | solution.py:472
  95.2 1.9 %shard_map.129 = (bf16[128,256]{1,0:T(8,128)(2,1)}, bf16[128,256]{1,0:T(8,128)(2,1)}, f32[256,256]{1,0:T(8,128)}, f32[256,256]{1,0:T(8,128)}, f32[1,256]{1,0:T(1,128)}) custom-call(bf16[128,256]{1,0:T(8,128)(2,1)} %get-tuple-element.15.refs_0_, bf16[128,256]{1,0:T(8,128)(2,1)} %get-tuple-element.16.refs_1_, f32[256,256]{1,0:T(8,128)} %get-tuple-element.17.refs_2_, ...), custom_call_target="tpu_custom_call" | custom-call | tf_op jit(solution)/shard_map/pallas_call | solution.py:531

commit v5 on v4

--- a/solution.py
+++ b/solution.py
@@ -37,9 +37,9 @@
 
 def kernel(
     rows_h, cols_h, count_h, feat_h, tiles_h, w_self_h, w_neigh_h, bias_h, cot_h,
-    out_h, gfeat_h, gself_h, gneigh_h, gbias_h,
+    out_h, gfeat_h, weights_h, gbias_h,
     A, T, X, PA, CR, Y, YR, ZS, ZR, TOT, G, ACC, BP, XR, XS, LR,
-    W, M, MC, M1, MX, M2, MY, M3, ML, M4, MH, R,
+    LEFT, W, M, MC, M1, MX, M2, MY, M3, ML, M4, MH, R,
     w_self, w_neigh, bias, cot, out, gfeat, gbias, rows_in, cols_in, count_in, table, inv,
     lsem, osem, s1z, r1z, s1x, r1x, s3c, r3c, s3y, r3y, s3z, r3z,
     s5z, r5z, s5y, r5y, s5c, r5c, s6x, r6x, s6l, r6l, sw, rw,
@@ -97,10 +97,11 @@
         return remote(src, dst, s3z.at[n], r3z.at[n], to_zh(1 + 2 * (n % 2)))
 
     def z5(k):
-        if k < 2:
+        if k in (2, 3):
+            block = G.at[mod4(zh + 3 - 2 * (k % 2)), c, y]
+        else:
             block = G.at[zh, c, y]
-        else:
-            block = half(G.at[mod4(zh + 3 - 2 * (k % 2)), c, y], k % 2)
+        block = half(block, (k + k // 4) % 2)
         return remote(block, block, s5z.at[k], r5z.at[k], to_zh(1 + 2 * (k % 2)))
 
     def y5(g, d):
@@ -269,13 +270,9 @@
     grad_pre_b = grad_pre.astype(BF)
     G[zh, c, y] = lax.dot_general(grad_pre_b, w_neigh[...], NT, preferred_element_type=F32).astype(BF)
 
-    z5(0).start()
-    z5(1).start()
+    for k in (0, 1, 4, 5):
+        z5(k).start()
     each3(lambda d: y5(0, d).start())
-    out[...] = (preact * sigma).astype(BF)
-    save_out = pltpu.make_async_copy(out, out_h, osem.at[0])
-    save_out.start()
-
     def split(value):
         high = value.astype(BF).astype(F32)
         return jnp.concatenate([high, value - high], axis=0).astype(BF)
@@ -292,26 +289,36 @@
     def wide(value):
         return value.astype(F32)
 
-    W[0:256] = lax.dot_general(X[i], grad_pre_b, TN, preferred_element_type=F32)
-    W[256:512] = lax.dot_general(aggregate, grad_pre_b, TN, preferred_element_type=F32)
+    LEFT[0] = X[i]
+    LEFT[1] = aggregate
     column = jnp.sum(grad_pre, axis=0, keepdims=True)
     row_id = lax.broadcasted_iota(jnp.int32, (8, 128), 0)
     bias_tile = split(jnp.where(row_id == 0, column[:, :128], jnp.where(row_id == 1, column[:, 128:], 0.0)))
 
-    @pl.loop(0, 32)
-    def _(q):
-        part = W[pl.ds(pl.multiple_of(q * 16, 16), 16), :].astype(BF)
-        a, b = lax.div(q, 16), lax.rem(q, 16)
-        u, v = lax.div(b, 4), lax.rem(b, 4)
-        M[a, u, v, 0] = part[:, 0:128]
-        M[a, u, v, 1] = part[:, 128:256]
-        M[a, u, v, 2] = bias_tile
-
-    wc().start()
-    gfeat_own = lax.dot_general(grad_pre_b, w_self[...], NT, preferred_element_type=F32)
+    @pl.loop(0, 2)
+    def _(k):
+        a = lax.rem(oc + k, 2)
+        W[0:256] = lax.dot_general(LEFT[a], grad_pre_b, TN, preferred_element_type=F32)
+
+        @pl.loop(0, 4)
+        def _(u):
+            for v in range(4):
+                part = W[pl.ds(pl.multiple_of(u * 64 + v * 16, 16), 16), :].astype(BF)
+                M[a, u, v, 0] = part[:, 0:128]
+                M[a, u, v, 1] = part[:, 128:256]
+                M[a, u, v, 2] = bias_tile
+
+        @pl.when(k == 0)
+        def _():
+            wc().start()
+
     wc().wait_recv()
     keep(M1, wide(M[c]) + wide(MC[...]))
     each3(lambda d: wx(d).start())
+    out[...] = (preact * sigma).astype(BF)
+    save_out = pltpu.make_async_copy(out, out_h, osem.at[0])
+    save_out.start()
+    gfeat_own = lax.dot_general(grad_pre_b, w_self[...], NT, preferred_element_type=F32)
 
     each3(lambda d: wx(d).wait_recv())
     keep(M2, wide(M1[x]) + wide(MX[0]) + wide(MX[1]) + wide(MX[2]))
@@ -319,12 +326,16 @@
 
     @pl.loop(0, 4)
     def _(g):
-        for k in range(2):
-
-            @pl.when(g == k)
-            def _():
+        @pl.when(g == 0)
+        def _():
+            for k in range(2):
                 z5(k).wait_recv()
                 z5(2 + k).start()
+            z5(4).wait_recv()
+
+        @pl.when(g == 1)
+        def _():
+            z5(5).wait_recv()
 
         @pl.when(g == 2)
         def _():
@@ -407,29 +418,33 @@
     each3(lambda d: vy(d).wait_recv())
     vc().start()
 
-    def assemble(a):
-        @pl.loop(0, 16)
-        def _(q):
-            u, v = lax.div(q, 4), lax.rem(q, 4)
-            rows = pl.ds(pl.multiple_of(a * 256 + q * 16, 16), 16)
-            W[rows, :] = wide(jnp.concatenate([R[a, v, u, 0], R[a, v, u, 1]], axis=1)) * factor
-
-    assemble(c)
+    def save_weights(a):
+        @pl.loop(0, 4)
+        def _(u):
+            for v in range(4):
+                rows = pl.ds(pl.multiple_of(a * 256 + u * 64 + v * 16, 16), 16)
+                W[rows, :] = wide(jnp.concatenate([R[a, v, u, 0], R[a, v, u, 1]], axis=1)) * factor
+
+        return pltpu.make_async_copy(
+            W.at[pl.ds(pl.multiple_of(a * 256, 256), 256)], weights_h.at[pl.ds(pl.multiple_of(a * 256, 256), 256)],
+            osem.at[2 + a],
+        )
+
+    save_own = save_weights(c)
+    save_own.start()
     total = TOT[...] + gfeat_own
     for n in range(3):
         l6(n).wait_recv()
         total = total + LR[n].astype(F32)
     gfeat[...] = total.astype(BF)
+    save_gfeat = pltpu.make_async_copy(gfeat, gfeat_h, osem.at[1])
+    save_gfeat.start()
+    save_bias = pltpu.make_async_copy(gbias, gbias_h, osem.at[4])
+    save_bias.start()
     vc().wait_recv()
-    assemble(oc)
-    saves = [
-        pltpu.make_async_copy(gfeat, gfeat_h, osem.at[1]),
-        pltpu.make_async_copy(W.at[pl.ds(0, 256)], gself_h, osem.at[2]),
-        pltpu.make_async_copy(W.at[pl.ds(256, 256)], gneigh_h, osem.at[3]),
-        pltpu.make_async_copy(gbias, gbias_h, osem.at[4]),
-    ]
-    for save in saves:
-        save.start()
+    save_other = save_weights(oc)
+    save_other.start()
+    saves = [save_own, save_gfeat, save_bias, save_other]
 
     @pl.loop(0, 4)
     def _(n):
@@ -448,17 +463,19 @@
         for copy in (z1(d), l6(d - 1), wx(d), wy(d), wl(d), vy(d), vx(d)):
             copy.wait_send()
 
-    for copy in (wc(), vc(), wh(0), wh(1), wh(2), *map(z3, range(4)), *map(z5, range(4))):
+    for copy in (wc(), vc(), wh(0), wh(1), wh(2), *map(z3, range(4)), *map(z5, range(6))):
         copy.wait_send()
     save_out.wait()
     for save in saves:
         save.wait()
 
 
-def hand_over(*refs):
-    n = len(refs) // 2
-    for k in range(n):
-        refs[n + k][...] = refs[k][...]
+def hand_over(out, gfeat, weights, gbias, out_to, gfeat_to, gself_to, gneigh_to, gbias_to):
+    out_to[...] = out[...]
+    gfeat_to[...] = gfeat[...]
+    gself_to[...] = weights[0:256]
+    gneigh_to[...] = weights[256:512]
+    gbias_to[...] = gbias[...]
 
 
 def body(features, adj_tiles, tile_row, tile_col, tile_count, w_self, w_neigh, bias_vec, cotangent):
@@ -471,9 +488,9 @@
     )
     held = pl.pallas_call(
         kernel,
-        out_shape=results,
+        out_shape=(results[0], results[1], sds((512, 256), F32), results[4]),
         in_specs=[whole] * 9,
-        out_specs=(whole,) * 5,
+        out_specs=(whole,) * 4,
         scratch_shapes=[
             pltpu.VMEM((4096, 2048), BF),
             pltpu.VMEM((SLOTS + 1, 128, 128), BF),
@@ -491,6 +508,7 @@
             pltpu.VMEM((4, 3, 128, 256), BF),
             pltpu.VMEM((3, 128, 256), BF),
             pltpu.VMEM((3, 128, 256), BF),
+            pltpu.VMEM((2, 128, 256), BF),
             pltpu.VMEM((512, 256), F32),
             pltpu.VMEM((2, 4, 4, 3, 16, 128), BF),
             pltpu.VMEM((4, 4, 3, 16, 128), BF),
@@ -518,7 +536,7 @@
             dma((10,)), dma((5,)),
             dma((3,)), dma((3,)), dma((4, 3)), dma((4, 3)),
             dma((4,)), dma((4,)), dma((4, 3)), dma((4, 3)), dma((4,)), dma((4,)),
-            dma((4,)), dma((4,)), dma((4, 3)), dma((4, 3)), dma((4,)), dma((4,)),
+            dma((6,)), dma((6,)), dma((4, 3)), dma((4, 3)), dma((4,)), dma((4,)),
             dma((4, 3)), dma((4, 3)), dma((3,)), dma((3,)),
             dma((21,)), dma((21,)),
         ],
@@ -531,7 +549,7 @@
     out, gfeat, gself, gneigh, gbias = pl.pallas_call(
         hand_over,
         out_shape=results,
-        in_specs=[vmem] * 5,
+        in_specs=[vmem] * 4,
         out_specs=(vmem,) * 5,
     )(*held)
     return out, gfeat, gself, gneigh, gbias.reshape(256)

time: 97.2 us -> 96.1 us (0.989)
  Pallas kernels: 95.8 us -> 94.6 us
    pallas_call x2, Pallas kernels: 95.8 us -> 94.6 us  [the longest x1 92.7 us: body(): pl.pallas_call(kernel, out_shape=(results[0], results[1], sds((512, 256),...]
where the time goes in v5:
time: 96.1 us; the launch traced here: 95.9 us
  Pallas kernels  94.6 us (98%)
  between operations  1.29 us (1%)
    pallas_call x1, Pallas kernels, body(): pl.pallas_call(kernel, out_shape=(results[0], results[1], sds((512, 256),...  92.7 us
    pallas_call x1, Pallas kernels, body(): pl.pallas_call(hand_over, out_shape=results, in_specs=[vmem] * 4, out_spe...  1.96 us

profile of v5, /device:TPU:1, one launch (start us, length us, event | category | flops | bytes accessed | tf_op | source)
XLA Modules:
  0.0 95.9 jit_solution(13559042698339950881)
XLA Ops:
  1.3 92.7 %shard_map.128 = (bf16[128,256]{1,0:T(8,128)(2,1)}, bf16[128,256]{1,0:T(8,128)(2,1)}, f32[512,256]{1,0:T(8,128)}, f32[1,256]{1,0:T(1,128)}) custom-call(s32[1,1,96]{2,1,0:T(1,128)} %rows_h.1, s32[1,1,96]{2,1,0:T(1,128)} %cols_h.1, s32[1,1]{1,0:T(1,128)S(6)} %copy.14.count_h, bf16[128,256]{1,0:T(8,128)(2,1)} %feat_h.1, bf16[1,1,96,128,128]{4,3,2,1,0:T(8,128)(2,1)} %tiles_h.1, ...), custom_call_target="tpu_custom_call" | custom-call | tf_op jit(solution)/shard_map/pallas_call | solution.py:489
  94.0 2.0 %shard_map.129 = (bf16[128,256]{1,0:T(8,128)(2,1)}, bf16[128,256]{1,0:T(8,128)(2,1)}, f32[256,256]{1,0:T(8,128)}, f32[256,256]{1,0:T(8,128)}, f32[1,256]{1,0:T(1,128)}) custom-call(bf16[128,256]{1,0:T(8,128)(2,1)} %get-tuple-element.14.out, bf16[128,256]{1,0:T(8,128)(2,1)} %get-tuple-element.15.gfeat, f32[512,256]{1,0:T(8,128)} %get-tuple-element.16.weights, ...), custom_call_target="tpu_custom_call" | custom-call | tf_op jit(solution)/shard_map/pallas_call | solution.py:549
